TPU v7x, 32 devices: a whole 2x2x4 slice. The times are simulated.
32 devices in a mesh: row: 8 (over y, x, core), col: 4 (over z).
Axes of the slice: x: 2, y: 2, z: 4, core: 2. Of those that a mesh axis runs over, the one named last changes fastest.
Arguments:
- features: bfloat16 [4096, 2048], P(('row', 'col')), may hold values from -20 to 20
- weight_one: bfloat16 [2048, 2048], replicated, may hold values from -0.25 to 0.25
- bias_one: float32 [2048], replicated, may hold values from -3 to 3
- weight_two: bfloat16 [2048, 2048], replicated, may hold values from -0.25 to 0.25
- bias_two: float32 [2048], replicated, may hold values from -3 to 3
- cotangent: bfloat16 [4096, 2048], P(('row', 'col')), may hold values from -6 to 6
- neighbours: int32 [4096, 16], P('row'), may hold values from -1 to 4095, as said below
- valid_mask: int32 [4096], P(('row', 'col')), may hold values from 0 to 1
Outputs:
- act: bfloat16 [4096, 2048], P(('row', 'col'))
- grad_input: bfloat16 [4096, 2048], P(('row', 'col'))
- grad_weight_one: float32 [2048, 2048], P(('row', 'col'))
- grad_bias_one: float32 [2048], P(('row', 'col'))
- grad_weight_two: float32 [2048, 2048], P(('row', 'col'))
- grad_bias_two: float32 [2048], P(('row', 'col'))
- rms_stats: float32 [2, 3], replicated
Inputs may be any that keep to these rules, and one draw needn't show every extreme that they name: `neighbours`: an entry is a node that row i aggregates, or -1 for an empty slot. No entry names a node whose valid_mask is 0, and the rows of such nodes hold only -1.
All inputs are finite; a program needn't handle non-finite values.
Results may differ from a plain program's by a relative error of at most 0.012.
The roundings to bfloat16 on the way count: a program that leaves them out, or rounds other values in their place, can miss the bound.
Values may be sent and summed in bfloat16 or wider, within the bound.
No kernel may reach another device: no remote copies, remote signals or barrier semaphores. Data moves between devices by JAX's collectives and lax.ppermute only.
A program may use at most 192 MiB of HBM per device.

v0:
```python
import jax
import jax.numpy as jnp
from jax import lax
from jax.sharding import PartitionSpec as P


def gelu_value(value):
    return jax.nn.gelu(value, approximate=True)


def source_parts(lists, per_dev, col_devs):
    live = lists >= 0
    safe = jnp.maximum(lists, 0)
    block = safe // per_dev
    return (live, block // col_devs, block % col_devs, safe % per_dev)


def count_tile(lists, usable, local_index, span):
    columns = jnp.arange(span, dtype=jnp.int32)[None, :]
    marked = jnp.where(usable, local_index, -1)
    total = jnp.zeros((lists.shape[0], span), jnp.float32)
    for slot in range(lists.shape[1]):
        total = total + (marked[:, slot : slot + 1] == columns).astype(jnp.float32)
    return total.astype(jnp.bfloat16)


def reduce_weights(grad_weight, grad_bias):
    return (
        lax.psum_scatter(grad_weight, ("row", "col"), scatter_dimension=0, tiled=True),
        lax.psum_scatter(grad_bias, ("row", "col"), scatter_dimension=0, tiled=True),
    )


def local(features, weight_one, bias_one, weight_two, bias_two, cotangent, neighbours, valid_mask):
    per_dev, width = features.shape
    row_devs = lax.axis_size("row")
    col_devs = lax.axis_size("col")
    col_pos = lax.axis_index("col")
    own_lists = lax.dynamic_slice_in_dim(neighbours, col_pos * per_dev, per_dev, 0)
    inverse = 1.0 / (jnp.sum(own_lists >= 0, axis=1).astype(jnp.float32) + 1.0)
    scaling = inverse[:, None]
    validity = valid_mask.astype(jnp.float32)[:, None]
    live, src_row, src_col, offset = source_parts(neighbours, per_dev, col_devs)
    front_tile = count_tile(
        neighbours, live & (src_col == col_pos), src_row * per_dev + offset, row_devs * per_dev
    )

    def forward_layer(inputs, weight, bias):
        gathered = lax.all_gather(inputs, "row", axis=0, tiled=True)
        partial_value = jnp.dot(front_tile, gathered, preferred_element_type=jnp.float32)
        summed = lax.psum_scatter(partial_value, "col", scatter_dimension=0, tiled=True)
        aggregate = ((summed + 2.0 * inputs.astype(jnp.float32)) * scaling).astype(jnp.bfloat16)
        preact = jnp.dot(aggregate, weight, preferred_element_type=jnp.float32) + bias
        return (aggregate, preact, validity * gelu_value(preact))

    agg_one, pre_one, out_one = forward_layer(features, weight_one, bias_one)
    hidden = out_one.astype(jnp.bfloat16)
    agg_two, pre_two, out_two = forward_layer(hidden, weight_two, bias_two)

    def squares(value):
        return jnp.sum(validity * jnp.square(value.astype(jnp.float32)))

    local_squares = jnp.stack(
        [
            squares(features),
            squares(agg_one),
            squares(out_one),
            squares(hidden),
            squares(agg_two),
            squares(out_two),
        ]
    ).reshape(2, 3)
    total_squares, total_valid = lax.psum((local_squares, jnp.sum(validity)), ("row", "col"))
    rms_stats = jnp.sqrt(total_squares / (total_valid * width) + 1e-06)

    def backward_layer(upstream, aggregate, preact, weight):
        grad_act = validity * upstream
        grad_pre = jax.vjp(gelu_value, preact)[1](grad_act)[0].astype(jnp.bfloat16)
        grad_weight = lax.dot_general(
            aggregate, grad_pre, (((0,), (0,)), ((), ())), preferred_element_type=jnp.float32
        )
        grad_bias = jnp.sum(grad_pre.astype(jnp.float32), axis=0)
        grad_low = lax.dot_general(
            grad_pre, weight, (((1,), (1,)), ((), ())), preferred_element_type=jnp.float32
        ).astype(jnp.bfloat16)
        grad_agg = lax.optimization_barrier(grad_low).astype(jnp.float32)
        grad_sum = (grad_agg * scaling).astype(jnp.bfloat16)
        grad_all = lax.all_gather(grad_sum, "col", axis=0, tiled=True)
        from_lists = lax.psum_scatter(
            lax.dot_general(
                front_tile, grad_all, (((0,), (0,)), ((), ())), preferred_element_type=jnp.float32
            ),
            "row",
            scatter_dimension=0,
            tiled=True,
        )
        return (from_lists + 2.0 * grad_agg * scaling, grad_weight, grad_bias)

    grad_hidden, weight_grad_two, bias_grad_two = backward_layer(
        cotangent.astype(jnp.float32), agg_two, pre_two, weight_two
    )
    weight_grad_two, bias_grad_two = reduce_weights(weight_grad_two, bias_grad_two)
    grad_start, weight_grad_one, bias_grad_one = backward_layer(
        grad_hidden, agg_one, pre_one, weight_one
    )
    weight_grad_one, bias_grad_one = reduce_weights(weight_grad_one, bias_grad_one)
    return (
        out_two.astype(jnp.bfloat16),
        grad_start.astype(jnp.bfloat16),
        weight_grad_one,
        bias_grad_one,
        weight_grad_two,
        bias_grad_two,
        rms_stats,
    )


def solution(mesh):
    in_specs = (
        P(("row", "col"), None),
        P(),
        P(),
        P(),
        P(),
        P(("row", "col"), None),
        P("row", None),
        P(("row", "col")),
    )
    out_specs = (
        P(("row", "col"), None),
        P(("row", "col"), None),
        P(("row", "col"), None),
        P(("row", "col")),
        P(("row", "col"), None),
        P(("row", "col")),
        P(),
    )
    return jax.shard_map(local, mesh=mesh, in_specs=in_specs, out_specs=out_specs, check_vma=False)
```

profile of v0, /device:TPU:8, one launch (start us, length us, event | category | flops | bytes accessed | tf_op | source)
XLA Modules:
  0.0 1281.8 jit_solution(15852315463225599241)
XLA Ops:
  7.2 0.0 all-gather.5.cloned.1.call-start
  7.2 0.7 all-gather.5.cloned.1.call-update
  7.9 0.0 reduce-scatter.7.cloned.1.call-start
  8.0 0.8 fusion.35
  8.8 39.0 %all-gather.5.cloned.1.call-done = bf16[1024,2048]{1,0:T(8,128)(2,1)} async-done(((bf16[128,2048]{1,0:T(8,128)(2,1)}), bf16[1024,2048]{1,0:T(8,128)(2,1)}) %all-gather.5.cloned.1.call-update) | async-done | bytes 4194320 | tf_op jit(solution)/shard_map/all_gather | solution.py:49
  47.8 10.1 fusion.43
  57.9 0.0 reduce-scatter.7.cloned.1.call-update
  58.0 0.0 copy-start.5
  58.0 0.0 all-gather.7.cloned.1.call-start
  58.0 0.6 copy-done.7
  58.6 0.7 convert_reduce_fusion.2
  59.3 75.6 %reduce-scatter.7.cloned.1.call-done = f32[128,2048]{1,0:T(8,128)} async-done(((f32[512,2048]{1,0:T(8,128)}), f32[128,2048]{1,0:T(8,128)}) %reduce-scatter.7.cloned.1.call-update) | async-done | bytes 1048592 | tf_op jit(solution)/shard_map/reduce_scatter | solution.py:51
  134.9 1.4 fusion.2
  136.3 0.0 copy-done.5
  136.3 6.1 fusion.30
  142.4 0.0 all-gather.7.cloned.1.call-update
  142.4 0.0 reduce-scatter.9.cloned.1.call-start
  142.5 37.3 %all-gather.7.cloned.1.call-done = bf16[1024,2048]{1,0:T(8,128)(2,1)} async-done(((bf16[128,2048]{1,0:T(8,128)(2,1)}), bf16[1024,2048]{1,0:T(8,128)(2,1)}) %all-gather.7.cloned.1.call-update) | async-done | bytes 4194320 | tf_op jit(solution)/shard_map/all_gather | solution.py:49
  179.8 10.1 fusion.42
  189.9 0.0 reduce-scatter.9.cloned.1.call-update
  190.0 0.0 copy-start.4
  190.0 0.0 copy-start.6
  190.0 0.2 all-gather.9.cloned.1.call-start
  190.2 76.7 %reduce-scatter.9.cloned.1.call-done = f32[128,2048]{1,0:T(8,128)} async-done(((f32[512,2048]{1,0:T(8,128)}), f32[128,2048]{1,0:T(8,128)}) %reduce-scatter.9.cloned.1.call-update) | async-done | bytes 1048592 | tf_op jit(solution)/shard_map/reduce_scatter | solution.py:51
  266.9 0.0 copy-done.1
  266.9 1.5 fusion.7
  268.4 0.0 slice-start.1
  268.5 6.6 convert_reduce_fusion
  275.1 0.0 slice-done.1
  275.1 2.9 convolution_convert_fusion.1
  278.0 0.9 fusion.10
  278.9 0.0 all-gather.9.cloned.1.call-update
  278.9 0.0 reduce-scatter.11.cloned.1.call-start
  279.0 45.0 %all-gather.9.cloned.1.call-done = bf16[512,2048]{1,0:T(8,128)(2,1)} async-done(((bf16[128,2048]{1,0:T(8,128)(2,1)}), bf16[512,2048]{1,0:T(8,128)(2,1)}) %all-gather.9.cloned.1.call-update) | async-done | bytes 2097168 | tf_op jit(solution)/shard_map/all_gather | solution.py:88
  323.9 10.8 fusion.41
  334.7 0.0 reduce-scatter.11.cloned.1.call-update
  334.8 0.3 all-gather.11.cloned.1.call-start
  335.0 71.5 %reduce-scatter.11.cloned.1.call-done = f32[128,2048]{1,0:T(8,128)} async-done(((f32[1024,2048]{1,0:T(8,128)}), f32[128,2048]{1,0:T(8,128)}) %reduce-scatter.11.cloned.1.call-update) | async-done | bytes 1048592 | tf_op jit(solution)/shard_map/reduce_scatter | solution.py:89
  406.5 4.9 multiply_reduce_fusion
  411.4 6.3 convolution_convert_fusion
  417.7 0.9 fusion.13
  418.6 0.0 all-gather.11.cloned.1.call-update
  418.6 0.0 reduce-scatter.13.cloned.1.call-start
  418.7 44.4 %all-gather.11.cloned.1.call-done = bf16[512,2048]{1,0:T(8,128)(2,1)} async-done(((bf16[128,2048]{1,0:T(8,128)(2,1)}), bf16[512,2048]{1,0:T(8,128)(2,1)}) %all-gather.11.cloned.1.call-update) | async-done | bytes 2097168 | tf_op jit(solution)/shard_map/all_gather | solution.py:88
  463.1 10.8 fusion.40
  473.9 0.0 reduce-scatter.13.cloned.1.call-update
  473.9 0.0 reduce-scatter.17.cloned.1.call-start
  473.9 1.0 copy-done.3
  474.9 10.0 fusion.48
  484.9 0.0 reduce-scatter.17.cloned.1.call-update
  485.0 0.3 reduce-scatter.15.cloned.1.call-start
  485.3 9.0 fusion.47
  494.3 0.0 reduce-scatter.15.cloned.1.call-update
  494.3 0.7 convert_reduce_fusion.3
  494.9 3.9 stack.27
  498.9 0.1 reshape.25
  499.0 41.7 %all-reduce.2 = (f32[2048]{0:T(1024)S(1)}, f32[2048]{0:T(1024)S(1)}, f32[2,3]{1,0:T(2,128)S(1)}, f32[]{:T(128)}) all-reduce(f32[2048]{0:T(1024)S(1)} %get-tuple-element.23, f32[2048]{0:T(1024)S(1)} %get-tuple-element.17, f32[2,3]{1,0:T(2,128)S(1)} %reshape.25, ...), channel_id=7, replica_groups=mesh['row'=8,'col'=4] {'row','col'}, use_global_device_ids=true, to_apply=%region_7.8.clone | all-reduce | flops 4103 | bytes 32824
  540.7 0.6 dynamic-slice
  541.2 0.6 dynamic-slice.1
  542.5 0.6 add_sqrt_fusion
  543.1 3.9 reduce-scatter.13.cloned.1.call-done
  547.0 2.2 fusion.15
  549.2 360.9 %reduce-scatter.17.cloned.1.call-done = f32[64,2048]{1,0:T(8,128)} async-done(((f32[2048,2048]{1,0:T(8,128)}), f32[64,2048]{1,0:T(8,128)}) %reduce-scatter.17.cloned.1.call-update) | async-done | bytes 524304 | tf_op jit(solution)/shard_map/reduce_scatter | solution.py:29
  910.1 364.9 %reduce-scatter.15.cloned.1.call-done = f32[64,2048]{1,0:T(8,128)} async-done(((f32[2048,2048]{1,0:T(8,128)}), f32[64,2048]{1,0:T(8,128)}) %reduce-scatter.15.cloned.1.call-update) | async-done | bytes 524304 | tf_op jit(solution)/shard_map/reduce_scatter | solution.py:29
  (15 shorter events, 0.1 us)
Async XLA Ops:
  7.2 40.6 %all-gather.5.cloned.1.call-start = ((), (), s32[]{:S(2)}) async-start(), calls=%async_computation.6 | async-start | bytes 4718592 | tf_op jit(solution)/shard_map/all_gather | solution.py:49
  7.9 127.0 %reduce-scatter.7.cloned.1.call-start = ((), (), s32[]{:S(2)}) async-start(), calls=%async_computation.7 | async-start | bytes 5242880 | tf_op jit(solution)/shard_map/reduce_scatter | solution.py:51
  57.9 0.7 copy-start.7
  57.9 77.0 %copy-start = (bf16[128,2048]{1,0:T(8,128)(2,1)S(1)}, bf16[128,2048]{1,0:T(8,128)(2,1)}, u32[]{:S(2)}) copy-start(bf16[128,2048]{1,0:T(8,128)(2,1)} %param.8) | copy-start | bytes 1572868
  58.0 78.3 %copy-start.5 = (f32[2048]{0:T(1024)S(1)}, f32[2048]{0:T(1024)}, u32[]{:S(2)}) copy-start(f32[2048]{0:T(1024)} %param.10) | copy-start | bytes 24580
  58.0 121.8 %all-gather.7.cloned.1.call-start = ((), (), s32[]{:S(2)}) async-start(), calls=%async_computation.8 | async-start | bytes 4718592 | tf_op jit(solution)/shard_map/all_gather | solution.py:49
  142.4 124.4 %reduce-scatter.9.cloned.1.call-start = ((), (), s32[]{:S(2)}) async-start(), calls=%async_computation.9 | async-start | bytes 5242880 | tf_op jit(solution)/shard_map/reduce_scatter | solution.py:51
  189.9 76.9 %copy-start.1 = (bf16[128,2048]{1,0:T(8,128)(2,1)S(1)}, bf16[128,2048]{1,0:T(8,128)(2,1)}, u32[]{:S(2)}) copy-start(bf16[128,2048]{1,0:T(8,128)(2,1)} %get-tuple-element.42) | copy-start | bytes 1572868
  190.0 78.5 %copy-start.4 = (bf16[128,2048]{1,0:T(8,128)(2,1)S(1)}, bf16[128,2048]{1,0:T(8,128)(2,1)}, u32[]{:S(2)}) copy-start(bf16[128,2048]{1,0:T(8,128)(2,1)} %param.13) | copy-start | bytes 1572868
  190.0 78.5 %copy-start.6 = (f32[2048]{0:T(1024)S(1)}, f32[2048]{0:T(1024)}, u32[]{:S(2)}) copy-start(f32[2048]{0:T(1024)} %param.12) | copy-start | bytes 24580
  190.0 134.0 %all-gather.9.cloned.1.call-start = ((), (), s32[]{:S(2)}) async-start(), calls=%async_computation.10 | async-start | bytes 2621440 | tf_op jit(solution)/shard_map/all_gather | solution.py:88
  266.9 8.2 slice-start
  268.4 6.6 slice-start.1
  275.1 2.9 copy-start.2
  278.9 127.6 %reduce-scatter.11.cloned.1.call-start = ((), (), s32[]{:S(2)}) async-start(), calls=%async_computation.11 | async-start | bytes 9437184 | tf_op jit(solution)/shard_map/reduce_scatter | solution.py:89
  334.8 128.3 %all-gather.11.cloned.1.call-start = ((), (), s32[]{:S(2)}) async-start(), calls=%async_computation.12 | async-start | bytes 2621440 | tf_op jit(solution)/shard_map/all_gather | solution.py:88
  418.6 128.4 %reduce-scatter.13.cloned.1.call-start = ((), (), s32[]{:S(2)}) async-start(), calls=%async_computation.13 | async-start | bytes 9437184 | tf_op jit(solution)/shard_map/reduce_scatter | solution.py:89
  473.9 1.0 copy-start.3
  473.9 436.2 %reduce-scatter.17.cloned.1.call-start = ((), (), s32[]{:S(2)}) async-start(), calls=%async_computation.15 | async-start | bytes 17301504 | tf_op jit(solution)/shard_map/reduce_scatter | solution.py:29
  485.0 790.0 %reduce-scatter.15.cloned.1.call-start = ((), (), s32[]{:S(2)}) async-start(), calls=%async_computation.14 | async-start | bytes 17301504 | tf_op jit(solution)/shard_map/reduce_scatter | solution.py:29
Sparse Core Ops, SparseCore 0:
  9.9 37.8 all-gather.4
  58.1 76.7 reduce-scatter.6
  142.6 37.2 all-gather.6
  190.1 76.7 reduce-scatter.8
  279.1 44.8 all-gather.8
  334.9 71.5 reduce-scatter.10
  418.7 44.3 all-gather.10
  474.0 72.9 reduce-scatter.12
  549.9 360.1 reduce-scatter.16
  912.8 362.1 reduce-scatter.14
where the time goes:
time: 1290 us; the launch traced here: 1280 us
  waiting for transfers between devices  1120 us (87%)
  matrix products  82.7 us (6%)
  blocking collectives  41.7 us (3%)
  between operations  14.9 us (1%)
  other arithmetic  14.7 us (1%)
    reduce_scatter x2, waiting for transfers between devices, reduce_weights(): lax.psum_scatter(grad_weight, ('row', 'col'), scatter_dimension=0, tiled=...  726 us
    reduce_scatter x2, waiting for transfers between devices, forward_layer(): lax.psum_scatter(partial_value, 'col', scatter_dimension=0, tiled=True)  152 us
    all_gather x2, waiting for transfers between devices, backward_layer(): grad_all = lax.all_gather(grad_sum, 'col', axis=0, tiled=True)  89.4 us
    all_gather x2, waiting for transfers between devices, forward_layer(): gathered = lax.all_gather(inputs, 'row', axis=0, tiled=True)  76.3 us
    reduce_scatter x2, waiting for transfers between devices, backward_layer(): lax.psum_scatter(lax.dot_general(front_tile, grad_all, (((0,), (0,)), (()...  75.4 us
    unnamed x1, blocking collectives  41.7 us
  transfers between devices with their start and end apart: 10, of which 10 were waited for; matrix products, arithmetic and copies ran while one was open for 2% of the time, Pallas kernels for 0%

commit v1 on v0

--- a/solution.py
+++ b/solution.py
@@ -1,7 +1,19 @@
+import functools
+
 import jax
 import jax.numpy as jnp
 from jax import lax
+from jax.experimental import pallas as pl
+from jax.experimental.pallas import tpu as pltpu
+from jax.sharding import Mesh
 from jax.sharding import PartitionSpec as P
+
+BF16, F32 = jnp.bfloat16, jnp.float32
+LANES = 128
+MXU = 256
+MIB = 1 << 20
+NT = (((1,), (1,)), ((), ()))
+GELU_C, GELU_A = 0.7978845608, 0.044715
 
 
 def gelu_value(value):
@@ -31,7 +43,7 @@
     )
 
 
-def local(features, weight_one, bias_one, weight_two, bias_two, cotangent, neighbours, valid_mask):
+def general(features, weight_one, bias_one, weight_two, bias_two, cotangent, neighbours, valid_mask):
     per_dev, width = features.shape
     row_devs = lax.axis_size("row")
     col_devs = lax.axis_size("col")
@@ -115,24 +127,451 @@
     )
 
 
+def halves(value):
+    high = value.astype(BF16)
+    return high, (value - high.astype(F32)).astype(BF16)
+
+
+def tile_kernel(high_ref, low_ref, tile_ref, inverse_ref):
+    groups, lanes = high_ref.shape
+    sources = tile_ref.shape[1]
+    rows = tile_ref.shape[0] // groups
+    place = lax.broadcasted_iota(jnp.int32, (MXU, lanes), 0)
+    for group in range(groups):
+        high = (place == high_ref[group : group + 1, :]).astype(F32).astype(BF16)
+        low = (place == low_ref[group : group + 1, :]).astype(F32).astype(BF16)
+        counts = lax.dot_general(high, low, NT, preferred_element_type=F32)
+        at = slice(group * rows, (group + 1) * rows)
+        total = jnp.zeros((rows, MXU), F32)
+        for block in range(sources // MXU):
+            piece = counts[block * rows : (block + 1) * rows]
+            tile_ref[at, block * MXU : (block + 1) * MXU] = piece.astype(BF16)
+            total = total + piece
+        degree = jnp.sum(total, axis=1, keepdims=True)
+        inverse_ref[at, :] = jnp.broadcast_to(1.0 / (degree + 1.0), (rows, LANES))
+
+
+def count_tiles(high, low, sources):
+    groups, lanes = high.shape
+    rows = MXU * MXU // sources
+    step = 8
+    return pl.pallas_call(
+        tile_kernel,
+        grid=(groups // step,),
+        in_specs=[pl.BlockSpec((step, lanes), lambda g: (g, 0))] * 2,
+        out_specs=[
+            pl.BlockSpec((step * rows, sources), lambda g: (g, 0)),
+            pl.BlockSpec((step * rows, LANES), lambda g: (g, 0)),
+        ],
+        out_shape=[
+            jax.ShapeDtypeStruct((groups * rows, sources), BF16),
+            jax.ShapeDtypeStruct((groups * rows, LANES), F32),
+        ],
+        cost_estimate=pl.CostEstimate(
+            flops=2 * groups * MXU * MXU * lanes,
+            bytes_accessed=2 * groups * rows * sources,
+            transcendentals=0,
+        ),
+    )(high, low)
+
+
+def forward_kernel(tile_ref, own_ref, other_ref, rows_ref, inverse_ref, out_ref):
+    half = own_ref.shape[0]
+    total = jnp.dot(tile_ref[:, :half], own_ref[...], preferred_element_type=F32)
+    total += jnp.dot(tile_ref[:, half:], other_ref[...], preferred_element_type=F32)
+    total += 2.0 * rows_ref[...].astype(F32)
+    out_ref[...] = (total * inverse_ref[...]).astype(BF16)
+
+
+def apply_forward(tile, own, other, inverse):
+    half, sources = tile.shape
+    width = own.shape[1]
+    step = half // 4
+    return pl.pallas_call(
+        forward_kernel,
+        grid=(half // step,),
+        in_specs=[
+            pl.BlockSpec((step, sources), lambda i: (i, 0)),
+            pl.BlockSpec((half, width), lambda i: (0, 0)),
+            pl.BlockSpec((half, width), lambda i: (0, 0)),
+            pl.BlockSpec((step, width), lambda i: (i, 0)),
+            pl.BlockSpec((step, width), lambda i: (i, 0)),
+        ],
+        out_specs=pl.BlockSpec((step, width), lambda i: (i, 0)),
+        out_shape=jax.ShapeDtypeStruct((half, width), BF16),
+        cost_estimate=pl.CostEstimate(
+            flops=4 * half * sources * width, bytes_accessed=2 * half * sources, transcendentals=0
+        ),
+    )(tile, own, other, own, inverse)
+
+
+def backward_kernel(with_more, grad_ref, tile_ref, *refs):
+    out_ref = refs[-1]
+    grads = jnp.concatenate([grad_ref[i] for i in range(grad_ref.shape[0])], axis=1)
+    total = jnp.dot(grads, tile_ref[...], preferred_element_type=F32)
+    for at in range(out_ref.shape[0]):
+        piece = total[:, at * LANES : (at + 1) * LANES]
+        if with_more:
+            piece = piece + refs[0][at].astype(F32)
+        out_ref[at] = piece.astype(BF16)
+
+
+def apply_backward(tile, grads, part, more=None):
+    half, sources = tile.shape
+    chips, width, nodes = grads.shape
+    steps = 4
+    block = chips // steps
+    specs = [
+        pl.BlockSpec((chips, width, nodes), lambda i: (0, 0, 0)),
+        pl.BlockSpec((half, half // steps), lambda i: (0, part * steps + i)),
+    ]
+    operands = [grads, tile]
+    if more is not None:
+        specs.append(pl.BlockSpec((block, width, nodes), lambda i: (i, 0, 0)))
+        operands.append(more)
+    return pl.pallas_call(
+        functools.partial(backward_kernel, more is not None),
+        grid=(steps,),
+        in_specs=specs,
+        out_specs=pl.BlockSpec((block, width, nodes), lambda i: (i, 0, 0)),
+        out_shape=jax.ShapeDtypeStruct((chips, width, nodes), BF16),
+        cost_estimate=pl.CostEstimate(
+            flops=4 * half * half * width, bytes_accessed=2 * half * half, transcendentals=0
+        ),
+    )(*operands)
+
+
+def dense_kernel(last, agg_ref, weight_ref, bias_ref, valid_ref, input_ref, out_ref, slope_ref, stat_ref):
+    step = pl.program_id(0)
+    valid = valid_ref[...]
+    agg = jnp.concatenate([agg_ref[i] for i in range(agg_ref.shape[0])], axis=1)
+    pre = jnp.dot(agg, weight_ref[...], preferred_element_type=F32) + bias_ref[...]
+    square = pre * pre
+    bend = jnp.tanh(GELU_C * (pre + GELU_A * (square * pre)))
+    out = valid * (0.5 * pre * (1.0 + bend))
+    inner = GELU_C * (1.0 + 3.0 * GELU_A * square)
+    slope_ref[...] = valid * (0.5 * (1.0 + bend) + 0.5 * pre * (1.0 - bend * bend) * inner)
+    low = out.astype(BF16)
+    if last:
+        out_ref[...] = low
+    else:
+        for at in range(out_ref.shape[0]):
+            out_ref[at] = low[:, at * LANES : (at + 1) * LANES]
+
+    def squares(value):
+        value = value.astype(F32)
+        return jnp.sum(valid * (value * value), axis=0, keepdims=True)
+
+    def lanes(value):
+        return sum(value[:, i : i + LANES] for i in range(0, value.shape[1], LANES))
+
+    @pl.when(step == 0)
+    def _():
+        stat_ref[...] = jnp.zeros_like(stat_ref)
+        stat_ref[1:2, :] = lanes(squares(agg))
+        stat_ref[4:5, :] = jnp.sum(jnp.broadcast_to(valid, (valid.shape[0], LANES)), axis=0, keepdims=True)
+
+    stat_ref[0:1, :] += lanes(squares(input_ref[...]))
+    stat_ref[2:3, :] += lanes(squares(out))
+    stat_ref[3:4, :] += lanes(squares(low))
+
+
+def dense_layer(agg, weight, bias, valid, inputs, last):
+    chips, nodes, width = agg.shape
+    full = weight.shape[1]
+    steps = 4
+    block = full // steps
+    if last:
+        out_spec = pl.BlockSpec((nodes, block), lambda f: (0, f))
+        out_shape = jax.ShapeDtypeStruct((nodes, full), BF16)
+        input_spec = pl.BlockSpec((nodes, LANES), lambda f: (0, 0))
+    else:
+        out_spec = pl.BlockSpec((chips // steps, nodes, width), lambda f: (f, 0, 0))
+        out_shape = jax.ShapeDtypeStruct((chips, nodes, width), BF16)
+        input_spec = pl.BlockSpec((nodes, block), lambda f: (0, f))
+    return pl.pallas_call(
+        functools.partial(dense_kernel, last),
+        grid=(steps,),
+        in_specs=[
+            pl.BlockSpec((chips, nodes, width), lambda f: (0, 0, 0)),
+            pl.BlockSpec((full, block), lambda f: (0, f)),
+            pl.BlockSpec((1, block), lambda f: (0, f)),
+            pl.BlockSpec((nodes, 1), lambda f: (0, 0)),
+            input_spec,
+        ],
+        out_specs=[
+            out_spec,
+            pl.BlockSpec((nodes, block), lambda f: (0, f)),
+            pl.BlockSpec((8, LANES), lambda f: (0, 0)),
+        ],
+        out_shape=[
+            out_shape,
+            jax.ShapeDtypeStruct((nodes, full), F32),
+            jax.ShapeDtypeStruct((8, LANES), F32),
+        ],
+        cost_estimate=pl.CostEstimate(
+            flops=2 * nodes * full * full, bytes_accessed=2 * full * full, transcendentals=nodes * full
+        ),
+    )(agg, weight, bias, valid, inputs)
+
+
+def gradient_kernel(first, slope_ref, weight_ref, inverse_ref, *refs):
+    (up_ref, extra_ref, other_ref), (pre_ref, agg_ref, sums_ref) = refs[:3], refs[3:]
+    full = slope_ref.shape[1]
+    inverse = inverse_ref[...]
+
+    @pl.when(pl.program_id(0) == 0)
+    def _():
+        if first:
+            for at in range(up_ref.shape[0]):
+                here = slice(at * LANES, (at + 1) * LANES)
+                up = up_ref[at].astype(F32) + 2.0 * extra_ref[at].astype(F32) * inverse
+                pre_ref[:, here] = (up.T * slope_ref[:, here]).astype(BF16)
+            pre_ref[:, full:] = jnp.zeros((pre_ref.shape[0], LANES), BF16)
+        else:
+            pre_ref[:, :full] = (up_ref[...].astype(F32) * slope_ref[...]).astype(BF16)
+            one = jnp.sum(extra_ref[...], axis=1, keepdims=True)
+            two = jnp.sum(other_ref[...], axis=1, keepdims=True)
+            row = lax.broadcasted_iota(jnp.int32, (8, 1), 0)
+
+            def pick(value, at, to):
+                return jnp.where(row == to, jnp.sum(jnp.where(row == at, value, 0.0), axis=0, keepdims=True), 0.0)
+
+            total = pick(one, 0, 0) + pick(one, 1, 1) + pick(one, 2, 2) + pick(one, 3, 3)
+            total += pick(two, 1, 4) + pick(two, 2, 5) + pick(one * (1.0 / LANES), 4, 6)
+            high = total.astype(BF16).astype(F32)
+            both = jnp.concatenate([high, total - high], axis=0)
+            rest = jnp.zeros((pre_ref.shape[0] - 16, LANES), BF16)
+            pre_ref[:16, full:] = jnp.broadcast_to(both, (16, LANES)).astype(BF16)
+            pre_ref[16:, full:] = rest
+
+    grads = lax.dot_general(weight_ref[...], pre_ref[:, :full], NT, preferred_element_type=F32)
+    low = grads.astype(BF16)
+    sums = (low.astype(F32) * inverse).astype(BF16)
+    for at in range(agg_ref.shape[0]):
+        agg_ref[at] = low[at * LANES : (at + 1) * LANES]
+        sums_ref[at] = sums[at * LANES : (at + 1) * LANES]
+
+
+def gradient_layer(slope, weight, inverse, upstream, extra, other, first):
+    nodes, full = slope.shape
+    steps = 4
+    block = full // steps
+    chips = full // LANES
+    whole = lambda value: pl.BlockSpec(value.shape, lambda k: (0,) * value.ndim)
+    tiles = pl.BlockSpec((chips // steps, LANES, nodes), lambda k: (k, 0, 0))
+    return pl.pallas_call(
+        functools.partial(gradient_kernel, first),
+        grid=(steps,),
+        in_specs=[
+            whole(slope),
+            pl.BlockSpec((block, full), lambda k: (k, 0)),
+            whole(inverse),
+            whole(upstream),
+            whole(extra),
+            whole(other),
+        ],
+        out_specs=[pl.BlockSpec((nodes, full + LANES), lambda k: (0, 0)), tiles, tiles],
+        out_shape=[
+            jax.ShapeDtypeStruct((nodes, full + LANES), BF16),
+            jax.ShapeDtypeStruct((chips, LANES, nodes), BF16),
+            jax.ShapeDtypeStruct((chips, LANES, nodes), BF16),
+        ],
+        cost_estimate=pl.CostEstimate(
+            flops=2 * nodes * full * full, bytes_accessed=2 * full * full, transcendentals=0
+        ),
+    )(slope, weight, inverse, upstream, extra, other)
+
+
+def weight_kernel(row_ref, agg_ref, *refs):
+    parts, (out_ref, left_ref) = refs[:10], refs[10:]
+    row = row_ref[0]
+    cols, piece_rows, full = out_ref.shape
+    full -= LANES
+    nodes = parts[0].shape[0]
+    width = 2 * LANES
+    for mask in range(8):
+        for half in range(2):
+            block = agg_ref[row ^ mask, half]
+            left_ref[half * LANES : (half + 1) * LANES, mask * nodes : (mask + 1) * nodes] = block.T
+    left_ref[width:, :] = jnp.ones((16, left_ref.shape[1]), BF16)
+    order = [
+        [parts[0]], [parts[5]], [parts[1]], [parts[6]], [parts[2]], [parts[7]],
+        [parts[3], parts[4]], [parts[8], parts[9]],
+    ]
+    step = 512
+    bias = []
+    for at in range(0, full, step):
+        right = jnp.concatenate([ref[:, at : at + step] for group in order for ref in group], axis=0)
+        total = jnp.dot(left_ref[...], right, preferred_element_type=F32)
+        for col in range(cols):
+            out_ref[col, :, at : at + step] = total[col * piece_rows : (col + 1) * piece_rows].astype(BF16)
+        bias.append(total[width : width + 8])
+    bias = jnp.concatenate(bias, axis=1)
+    mine = jnp.zeros((8, width), F32)
+    for at in range(full // width):
+        mine += jnp.where(row == at, bias[:, at * width : (at + 1) * width], 0.0)
+    line = lax.broadcasted_iota(jnp.int32, (8, LANES), 0)
+    mine = jnp.where(line % 2 == 0, mine[:, :LANES], mine[:, LANES:])
+    mine_high = mine.astype(BF16).astype(F32)
+    mine = jnp.where(line < 2, mine_high, jnp.where(line < 4, mine - mine_high, 0.0))
+    stats = jnp.zeros((8, LANES), F32)
+    for group in order:
+        both = group[0][:16, full:].astype(F32)
+        stats += both[:8] + both[8:]
+    high = stats.astype(BF16).astype(F32)
+    rest = jnp.zeros((piece_rows - 24, LANES), F32)
+    extra = jnp.concatenate([mine, high, stats - high, rest], axis=0).astype(BF16)
+    for col in range(cols):
+        out_ref[col, :, full:] = extra
+
+
+def weight_product(row, aggs, parts, cols):
+    nodes, full = parts[0].shape
+    full -= LANES
+    rows = 2 * LANES // cols
+    vmem = pl.BlockSpec(memory_space=pltpu.VMEM)
+    return pl.pallas_call(
+        weight_kernel,
+        in_specs=[pl.BlockSpec(memory_space=pltpu.SMEM)] + [vmem] * 11,
+        out_specs=vmem,
+        out_shape=jax.ShapeDtypeStruct((cols, rows, full + LANES), BF16),
+        scratch_shapes=[pltpu.VMEM((2 * LANES + 16, 8 * nodes), BF16)],
+        cost_estimate=pl.CostEstimate(
+            flops=2 * 8 * nodes * full * 2 * LANES, bytes_accessed=2 * 8 * nodes * full, transcendentals=0
+        ),
+    )(row, aggs, *parts)
+
+
+def final_kernel(up_ref, agg_ref, inverse_ref, out_ref):
+    inverse = inverse_ref[...]
+    for at in range(up_ref.shape[0]):
+        value = up_ref[at].astype(F32) + 2.0 * agg_ref[at].astype(F32) * inverse
+        out_ref[:, at * LANES : (at + 1) * LANES] = value.T.astype(BF16)
+
+
+def input_gradient(upstream, grad_agg, inverse):
+    chips, width, nodes = upstream.shape
+    vmem = pl.BlockSpec(memory_space=pltpu.VMEM)
+    return pl.pallas_call(
+        final_kernel,
+        in_specs=[vmem] * 3,
+        out_specs=vmem,
+        out_shape=jax.ShapeDtypeStruct((nodes, chips * width), BF16),
+    )(upstream, grad_agg, inverse)
+
+
+def transposed(features, weight_one, bias_one, weight_two, bias_two, cotangent, neighbours, valid_mask):
+    nodes, full = features.shape
+    chip_rows, cols = lax.axis_size("ch"), lax.axis_size("col")
+    chips = chip_rows * cols
+    half = chips * nodes
+    sources = 2 * half
+    slots = neighbours.shape[1]
+    core = lax.axis_index("core")
+    col = lax.axis_index("col")
+    row = 2 * lax.axis_index("ch") + core
+    plane, every = ("ch", "core"), ("ch", "col")
+
+    def swap(value):
+        return lax.ppermute(value, "core", [(0, 1), (1, 0)])
+
+    def across(value, mask):
+        return lax.ppermute(value, "ch", [(i, i ^ mask) for i in range(chip_rows)])
+
+    def exchange(value):
+        return lax.all_to_all(value, every, 0, 0, tiled=True)
+
+    lists = neighbours.reshape(1, -1, MXU)
+    lists = jnp.broadcast_to(lists, (chip_rows,) + lists.shape[1:])
+    lists = lax.all_to_all(lists, "ch", 0, 0, tiled=True).reshape(-1, MXU)
+    live = lists >= 0
+    node = jnp.maximum(lists, 0)
+    owner, offset = node // nodes, node % nodes
+    owner_row, owner_col = owner // cols, owner % cols
+    place = ((owner_row // 2) * cols + owner_col) * nodes + offset
+    place = jnp.where(owner_row % 2 == core, place, place + half)
+    group_rows = MXU // slots
+    line = lax.broadcasted_iota(jnp.int32, lists.shape, 1) // slots
+    high = jnp.where(live, (place // MXU) * group_rows + line, -1)
+    tile, wide_inverse = count_tiles(high, place % MXU, sources)
+
+    own_lists = lax.dynamic_slice_in_dim(neighbours, col * nodes, nodes, 0)
+    inverse = 1.0 / (jnp.sum(own_lists >= 0, axis=1).astype(F32) + 1.0)
+    inverse = inverse.reshape(1, nodes)
+    valid = valid_mask.astype(F32).reshape(nodes, 1)
+
+    own = lax.all_to_all(features, every, 1, 0, tiled=True)
+    agg_one = apply_forward(tile, own, swap(own), wide_inverse)
+    agg_one = exchange(agg_one.reshape(chips, nodes, LANES))
+    hidden, slope_one, stats_one = dense_layer(agg_one, weight_one, bias_one.reshape(1, -1), valid, features, False)
+    own = exchange(hidden).reshape(half, LANES)
+    agg_two = apply_forward(tile, own, swap(own), wide_inverse)
+    agg_two = exchange(agg_two.reshape(chips, nodes, LANES))
+    act, slope_two, stats_two = dense_layer(agg_two, weight_two, bias_two.reshape(1, -1), valid, features, True)
+
+    def in_plane(aggs):
+        aggs = aggs.reshape(2 * chip_rows, -1, nodes, LANES)
+        return lax.all_to_all(aggs, plane, 0, 0, tiled=True)
+
+    def gather_plane(value):
+        by_x, by_y = across(value, 1), across(value, 2)
+        cut = nodes // 2
+        mine = [value, by_x, by_y, across(by_x[:cut], 2), across(by_y[cut:], 1)]
+        return mine + [swap(part) for part in mine]
+
+    def adjacency_backward(grads):
+        grads = exchange(grads)
+        more = swap(apply_backward(tile, grads, 1))
+        return exchange(apply_backward(tile, grads, 0, more))
+
+    def reduce_weight(aggs, grad_pre):
+        parts = weight_product(row.reshape(1), in_plane(aggs), gather_plane(grad_pre), cols)
+        parts = lax.all_to_all(parts, "col", 0, 0, tiled=True)
+        total = jnp.sum(parts.astype(F32), axis=0)
+        extra = total[:, full:]
+        bias = (extra[0:2] + extra[2:4]).reshape(-1)
+        count = full // (2 * chips)
+        bias = lax.dynamic_slice_in_dim(bias, col * count, count, 0)
+        return total[:, :full], bias, extra[8:16, 0] + extra[16:24, 0]
+
+    grad_pre_two, grad_agg_two, sums_two = gradient_layer(
+        slope_two, weight_two, inverse, cotangent, stats_one, stats_two, False
+    )
+    upstream = adjacency_backward(sums_two)
+    weight_grad_two, bias_grad_two, stats = reduce_weight(agg_two, grad_pre_two)
+    grad_pre_one, grad_agg_one, sums_one = gradient_layer(
+        slope_one, weight_one, inverse, upstream, grad_agg_two, stats_one, True
+    )
+    grad_start = input_gradient(adjacency_backward(sums_one), grad_agg_one, inverse)
+    weight_grad_one, bias_grad_one, _ = reduce_weight(agg_one, grad_pre_one)
+    rms_stats = jnp.sqrt(stats[:6].reshape(2, 3) / (stats[6] * full) + 1e-06)
+    return (act, grad_start, weight_grad_one, bias_grad_one, weight_grad_two, bias_grad_two, rms_stats)
+
+
 def solution(mesh):
-    in_specs = (
-        P(("row", "col"), None),
-        P(),
-        P(),
-        P(),
-        P(),
-        P(("row", "col"), None),
-        P("row", None),
-        P(("row", "col")),
-    )
-    out_specs = (
-        P(("row", "col"), None),
-        P(("row", "col"), None),
-        P(("row", "col"), None),
-        P(("row", "col")),
-        P(("row", "col"), None),
-        P(("row", "col")),
-        P(),
-    )
-    return jax.shard_map(local, mesh=mesh, in_specs=in_specs, out_specs=out_specs, check_vma=False)
+    rows, cols = mesh.devices.shape
+    axes = ("ch", "core", "col")
+    wide = Mesh(mesh.devices.reshape(rows // 2, 2, cols), axes)
+
+    def program(features, *rest):
+        nodes, full = features.shape
+        slots = rest[5].shape[1]
+        fits = (
+            (rows, cols) == (8, 4)
+            and nodes == rows * cols * LANES
+            and full == rows * cols * 64
+            and slots * nodes == MXU * MXU
+        )
+        split, over = (axes, wide) if fits else (("row", "col"), mesh)
+        lists = ("ch", "core") if fits else "row"
+        spread = P(split, None)
+        return jax.shard_map(
+            transposed if fits else general,
+            mesh=over,
+            in_specs=(spread, P(), P(), P(), P(), spread, P(lists, None), P(split)),
+            out_specs=(spread, spread, spread, P(split), spread, P(split), P()),
+            check_vma=False,
+        )(features, *rest)
+
+    return program

time: 1290 us -> 351 us (0.27)
  waiting for transfers between devices: 1120 us -> 103 us
  Pallas kernels: 0 us -> 100 us
  matrix products: 82.7 us -> 0 us
  starting transfers between devices: 1.07 us -> 65.4 us
  blocking collectives: 41.7 us -> 58.9 us
  between operations: 14.9 us -> 1.57 us
    reduce_scatter x6 -> x0, waiting for transfers between devices: 953 us -> none  [the longest x2 726 us: reduce_weights(): lax.psum_scatter(grad_weight, ('row', 'col'), scatter_dimension=0, tiled=...]
    all_gather x4 -> x0, waiting for transfers between devices: 166 us -> none  [the longest x2 89.4 us: backward_layer(): grad_all = lax.all_gather(grad_sum, 'col', axis=0, tiled=True)]
    pallas_call x0 -> x14, Pallas kernels: none -> 100 us  [the longest x4 24.5 us: apply_backward(): pl.pallas_call(functools.partial(backward_kernel, more is not None), grid...]
    dot_general x10 -> x0, matrix products: 82.7 us -> none  [the longest x2 21.6 us: backward_layer(): lax.dot_general(front_tile, grad_all, (((0,), (0,)), ((), ())), preferred...]
    all_to_all x0 -> x10, waiting for transfers between devices: none -> 71.1 us  [the longest x2 27.6 us: reduce_weight(): parts = lax.all_to_all(parts, 'col', 0, 0, tiled=True)]
    all_to_all x0 -> x3, blocking collectives: none -> 58.9 us  [exchange(): return lax.all_to_all(value, every, 0, 0, tiled=True)]
    all_to_all x0 -> x10, starting transfers between devices: none -> 55.5 us  [the longest x4 26.9 us: exchange(): return lax.all_to_all(value, every, 0, 0, tiled=True)]
    unnamed x1 -> x0, blocking collectives: 41.7 us -> none
  transfers between devices with their start and end apart: 10 -> 32, of which waited for: 10 -> 18; matrix products, arithmetic and copies ran while one was open for 2% -> 2% of each run, Pallas kernels for 0% -> 15%
where the time goes in v1:
time: 351 us; the launch traced here: 345 us
  waiting for transfers between devices  103 us (29%)
  Pallas kernels  100 us (28%)
  starting transfers between devices  65.4 us (19%)
  blocking collectives  58.9 us (17%)
  local copies, waits for them, and re-layouts  11.9 us (3%)
  other arithmetic  3.61 us (1%)
    all_to_all x3, blocking collectives, exchange(): return lax.all_to_all(value, every, 0, 0, tiled=True)  58.9 us
    all_to_all x2, waiting for transfers between devices, reduce_weight(): parts = lax.all_to_all(parts, 'col', 0, 0, tiled=True)  27.6 us
    all_to_all x4, starting transfers between devices, exchange(): return lax.all_to_all(value, every, 0, 0, tiled=True)  26.9 us
    all_to_all x4, waiting for transfers between devices, exchange(): return lax.all_to_all(value, every, 0, 0, tiled=True)  26 us
    ppermute x8, waiting for transfers between devices, across(): return lax.ppermute(value, 'ch', [(i, i ^ mask) for i in range(chip_rows)])  25.2 us
    pallas_call x4, Pallas kernels, apply_backward(): pl.pallas_call(functools.partial(backward_kernel, more is not None), grid...  24.5 us
    pallas_call x2, Pallas kernels, apply_forward(): pl.pallas_call(forward_kernel, grid=(half // step,), in_specs=[pl.BlockSp...  22 us
    pallas_call x2, Pallas kernels, gradient_layer(): pl.pallas_call(functools.partial(gradient_kernel, first), grid=(steps,),...  14.3 us
  transfers between devices with their start and end apart: 32, of which 18 were waited for; matrix products, arithmetic and copies ran while one was open for 2% of the time, Pallas kernels for 15%

profile of v1, /device:TPU:8, one launch (start us, length us, event | category | flops | bytes accessed | tf_op | source)
XLA Modules:
  0.0 344.8 jit_solution(2302155236890971098)
XLA Ops:
  0.6 0.9 copy.18
  1.7 0.7 broadcast_in_dim.10
  2.4 3.7 %all-to-all-start = ((s32[4,32,256]{2,1,0:T(8,128)}), s32[4,32,256]{2,1,0:T(8,128)S(1)}, u32[]{:S(2)}, u32[]{:S(2)}) async-start(s32[4,32,256]{2,1,0:T(8,128)} %broadcast_in_dim.10), calls=%async_computation | async-start | bytes 262144 | tf_op jit(solution)/shard_map/all_to_all | solution.py:487
  6.1 0.9 copy_bitcast_fusion
  7.1 4.1 %all-to-all-done = s32[4,32,256]{2,1,0:T(8,128)S(1)} async-done(((s32[4,32,256]{2,1,0:T(8,128)}), s32[4,32,256]{2,1,0:T(8,128)S(1)}, u32[]{:S(2)}, u32[]{:S(2)}) %all-to-all-start) | async-done | bytes 131104 | tf_op jit(solution)/shard_map/all_to_all | solution.py:487
  11.1 5.7 %all-to-all-start.1 = ((bf16[128,16,128]{2,0,1:T(8,128)(2,1)}), bf16[128,16,128]{2,0,1:T(8,128)(2,1)S(1)}, u32[]{:S(2)}, u32[]{:S(2)}) async-start(bf16[128,16,128]{2,0,1:T(8,128)(2,1)} %copy_bitcast_fusion), calls=%async_computation.1 | async-start | bytes 1048576 | tf_op jit(solution)/shard_map/all_to_all | solution.py:504
  17.0 1.0 add_select_fusion
  18.0 11.0 %all-to-all-done.1 = bf16[128,16,128]{2,0,1:T(8,128)(2,1)S(1)} async-done(((bf16[128,16,128]{2,0,1:T(8,128)(2,1)}), bf16[128,16,128]{2,0,1:T(8,128)(2,1)S(1)}, u32[]{:S(2)}, u32[]{:S(2)}) %all-to-all-start.1) | async-done | bytes 524320 | tf_op jit(solution)/shard_map/all_to_all | solution.py:504
  29.0 0.8 fusion.7.high_ref
  29.8 14.2 %shard_map.135 = (bf16[2048,4096]{1,0:T(8,128)(2,1)}, f32[2048,128]{1,0:T(8,128)}) custom-call(s32[128,256]{1,0:T(8,128)} %fusion.7.high_ref, s32[128,256]{1,0:T(8,128)} %get-tuple-element.35.low_ref), custom_call_target="tpu_custom_call" | custom-call | flops 4294967296 | bytes 16777216 | tf_op jit(solution)/shard_map/pallas_call | solution.py:158
  44.1 0.8 copy-done.16
  44.9 11.0 %shard_map.136 = bf16[2048,128]{1,0:T(8,128)(2,1)} custom-call(bf16[2048,4096]{1,0:T(8,128)(2,1)} %get-tuple-element.21.tile_ref, bf16[2048,128]{1,0:T(8,128)(2,1)} %bitcast.51, bf16[2048,128]{1,0:T(8,128)(2,1)} %copy-done.16, bf16[2048,128]{1,0:T(8,128)(2,1)} %bitcast.52, f32[2048,128]{1,0:T(8,128)} %get-tuple-element.22.inverse_ref), custom_call_target="tpu_custom_call" | custom-call | flops 4294967296 | bytes 16777216 | tf_op jit(solution)/shard_map/pallas_call | solution.py:190
  55.9 6.9 %all-to-all-start.2 = ((bf16[16,128,128]{2,1,0:T(8,128)(2,1)}), bf16[16,128,128]{2,1,0:T(8,128)(2,1)}, u32[]{:S(2)}, u32[]{:S(2)}) async-start(bf16[16,128,128]{2,1,0:T(8,128)(2,1)} %bitcast.57), calls=%async_computation.2 | async-start | bytes 1048576 | tf_op jit(solution)/shard_map/all_to_all | solution.py:483
  62.8 0.7 copy.20.valid_ref
  63.6 13.3 %all-to-all-done.2.agg_ref = bf16[16,128,128]{2,1,0:T(8,128)(2,1)} async-done(((bf16[16,128,128]{2,1,0:T(8,128)(2,1)}), bf16[16,128,128]{2,1,0:T(8,128)(2,1)}, u32[]{:S(2)}, u32[]{:S(2)}) %all-to-all-start.2) | async-done | bytes 524320 | tf_op jit(solution)/shard_map/all_to_all | solution.py:483
  76.9 6.8 %shard_map.137 = (bf16[16,128,128]{2,1,0:T(8,128)(2,1)}, f32[128,2048]{1,0:T(8,128)}, f32[8,128]{1,0:T(8,128)}) custom-call(bf16[16,128,128]{2,1,0:T(8,128)(2,1)} %all-to-all-done.2.agg_ref, bf16[2048,2048]{1,0:T(8,128)(2,1)} %weight_ref.7, f32[1,2048]{1,0:T(1,128)} %bitcast.58, f32[128,1]{1,0:T(8,128)} %copy.20.valid_ref, bf16[128,2048]{1,0:T(8,128)(2,1)} %input_ref.3), custom_call_target="tpu_custom_call" | custom-call | flops 1073741824 | bytes 8388608 | tf_op jit(solution)/shard_map/pallas_call | solution.py:292
  83.7 19.7 %all_to_all.79 = bf16[16,128,128]{2,1,0:T(8,128)(2,1)S(1)} all-to-all(bf16[16,128,128]{2,1,0:T(8,128)(2,1)} %get-tuple-element.23), channel_id=1, replica_groups=mesh['ch'=4,'core'=2,'col'=4] {'ch','col'}, dimensions={0} | all-to-all | bytes 1048576 | tf_op jit(solution)/shard_map/all_to_all | solution.py:483
  103.4 1.9 collective-permute-done.1.other_ref
  105.3 0.8 copy-done.19
  106.1 11.0 %shard_map.138 = bf16[2048,128]{1,0:T(8,128)(2,1)} custom-call(bf16[2048,4096]{1,0:T(8,128)(2,1)} %get-tuple-element.21.tile_ref, bf16[2048,128]{1,0:T(8,128)(2,1)} %bitcast.54, bf16[2048,128]{1,0:T(8,128)(2,1)} %copy-done.19, bf16[2048,128]{1,0:T(8,128)(2,1)} %bitcast.55, f32[2048,128]{1,0:T(8,128)} %get-tuple-element.22.inverse_ref), custom_call_target="tpu_custom_call" | custom-call | flops 4294967296 | bytes 16777216 | tf_op jit(solution)/shard_map/pallas_call | solution.py:190
  117.1 7.1 %all-to-all-start.4 = ((bf16[16,128,128]{2,1,0:T(8,128)(2,1)}), bf16[16,128,128]{2,1,0:T(8,128)(2,1)}, u32[]{:S(2)}, u32[]{:S(2)}) async-start(bf16[16,128,128]{2,1,0:T(8,128)(2,1)} %bitcast.56), calls=%async_computation.4 | async-start | bytes 1048576 | tf_op jit(solution)/shard_map/all_to_all | solution.py:483
  124.2 0.7 convert_reduce_fusion.2
  125.4 12.7 %all-to-all-done.4.agg_ref = bf16[16,128,128]{2,1,0:T(8,128)(2,1)} async-done(((bf16[16,128,128]{2,1,0:T(8,128)(2,1)}), bf16[16,128,128]{2,1,0:T(8,128)(2,1)}, u32[]{:S(2)}, u32[]{:S(2)}) %all-to-all-start.4) | async-done | bytes 524320 | tf_op jit(solution)/shard_map/all_to_all | solution.py:483
  138.1 6.7 %shard_map.139 = (bf16[128,2048]{1,0:T(8,128)(2,1)}, f32[128,2048]{1,0:T(8,128)}, f32[8,128]{1,0:T(8,128)}) custom-call(bf16[16,128,128]{2,1,0:T(8,128)(2,1)} %all-to-all-done.4.agg_ref, bf16[2048,2048]{1,0:T(8,128)(2,1)} %weight_ref.6, f32[1,2048]{1,0:T(1,128)} %bitcast.59, f32[128,1]{1,0:T(8,128)} %copy.20.valid_ref, bf16[128,2048]{1,0:T(8,128)(2,1)} %input_ref.3), custom_call_target="tpu_custom_call" | custom-call | flops 1073741824 | bytes 8388608 | tf_op jit(solution)/shard_map/pallas_call | solution.py:292
  144.8 7.1 %shard_map.140 = (bf16[128,2176]{1,0:T(8,128)(2,1)}, bf16[16,128,128]{2,1,0:T(8,128)(2,1)}, bf16[16,128,128]{2,1,0:T(8,128)(2,1)}) custom-call(f32[128,2048]{1,0:T(8,128)} %get-tuple-element.26.slope_ref, bf16[2048,2048]{1,0:T(8,128)(2,1)} %weight_ref.6, f32[1,128]{1,0:T(1,128)} %divide_bitcast_fusion.inverse_ref, bf16[128,2048]{1,0:T(8,128)(2,1)} %refs_0_.1, ...), custom_call_target="tpu_custom_call" | custom-call | flops 1073741824 | bytes 8388608 | tf_op jit(solution)/shard_map/pallas_call | solution.py:363
  151.9 19.9 %all_to_all.80.grad_ref = bf16[16,128,128]{2,1,0:T(8,128)(2,1)} all-to-all(bf16[16,128,128]{2,1,0:T(8,128)(2,1)} %get-tuple-element.29), channel_id=1, replica_groups=mesh['ch'=4,'core'=2,'col'=4] {'ch','col'}, dimensions={0} | all-to-all | bytes 1048576 | tf_op jit(solution)/shard_map/all_to_all | solution.py:483
  171.8 5.7 %shard_map.141 = bf16[16,128,128]{2,1,0:T(8,128)(2,1)} custom-call(bf16[16,128,128]{2,1,0:T(8,128)(2,1)} %all_to_all.80.grad_ref, bf16[2048,4096]{1,0:T(8,128)(2,1)} %get-tuple-element.21.tile_ref), custom_call_target="tpu_custom_call" | custom-call | flops 2147483648 | bytes 8388608 | tf_op jit(solution)/shard_map/pallas_call | solution.py:232
  177.5 3.5 %all-to-all-start.9 = ((bf16[8,2,128,128]{3,2,1,0:T(8,128)(2,1)}), bf16[8,2,128,128]{3,2,1,0:T(8,128)(2,1)S(1)}, u32[]{:S(2)}, u32[]{:S(2)}) async-start(bf16[8,2,128,128]{3,2,1,0:T(8,128)(2,1)} %bitcast.15), calls=%async_computation.9 | async-start | bytes 1048576 | tf_op jit(solution)/shard_map/all_to_all | solution.py:515
  181.0 0.8 copy-done.18
  181.8 6.5 %shard_map.142 = bf16[16,128,128]{2,1,0:T(8,128)(2,1)} custom-call(bf16[16,128,128]{2,1,0:T(8,128)(2,1)} %all_to_all.80.grad_ref, bf16[2048,4096]{1,0:T(8,128)(2,1)} %get-tuple-element.21.tile_ref, bf16[16,128,128]{2,1,0:T(8,128)(2,1)} %copy-done.18), custom_call_target="tpu_custom_call" | custom-call | flops 2147483648 | bytes 8388608 | tf_op jit(solution)/shard_map/pallas_call | solution.py:232
  188.3 2.4 all-to-all-done.9.agg_ref
  190.7 19.4 %all_to_all.81.refs_0_ = bf16[16,128,128]{2,1,0:T(8,128)(2,1)} all-to-all(bf16[16,128,128]{2,1,0:T(8,128)(2,1)} %shard_map.142), channel_id=1, replica_groups=mesh['ch'=4,'core'=2,'col'=4] {'ch','col'}, dimensions={0} | all-to-all | bytes 1048576 | tf_op jit(solution)/shard_map/all_to_all | solution.py:483
  210.0 3.5 %all-to-all-start.11 = ((bf16[8,2,128,128]{3,2,1,0:T(8,128)(2,1)}), bf16[8,2,128,128]{3,2,1,0:T(8,128)(2,1)S(1)}, u32[]{:S(2)}, u32[]{:S(2)}) async-start(bf16[8,2,128,128]{3,2,1,0:T(8,128)(2,1)} %bitcast.17), calls=%async_computation.11 | async-start | bytes 1048576 | tf_op jit(solution)/shard_map/all_to_all | solution.py:515
  213.5 1.9 collective-permute-start.14
  215.5 1.5 collective-permute-start.13
  217.0 7.3 %shard_map.143 = (bf16[128,2176]{1,0:T(8,128)(2,1)}, bf16[16,128,128]{2,1,0:T(8,128)(2,1)}, bf16[16,128,128]{2,1,0:T(8,128)(2,1)}) custom-call(f32[128,2048]{1,0:T(8,128)} %get-tuple-element.25.slope_ref, bf16[2048,2048]{1,0:T(8,128)(2,1)} %weight_ref.7, f32[1,128]{1,0:T(1,128)} %divide_bitcast_fusion.inverse_ref, bf16[16,128,128]{2,1,0:T(8,128)(2,1)} %all_to_all.81.refs_0_, ...), custom_call_target="tpu_custom_call" | custom-call | flops 1073741824 | bytes 8388608 | tf_op jit(solution)/shard_map/pallas_call | solution.py:363
  224.2 6.2 %all-to-all-start.7 = ((bf16[16,128,128]{2,1,0:T(8,128)(2,1)}), bf16[16,128,128]{2,1,0:T(8,128)(2,1)S(1)}, u32[]{:S(2)}, u32[]{:S(2)}) async-start(bf16[16,128,128]{2,1,0:T(8,128)(2,1)} %get-tuple-element.31), calls=%async_computation.7 | async-start | bytes 1048576 | tf_op jit(solution)/shard_map/all_to_all | solution.py:483
  230.5 4.7 %collective-permute-done.14.refs_2_ = bf16[128,2176]{1,0:T(8,128)(2,1)S(1)} collective-permute-done((bf16[128,2176]{1,0:T(8,128)(2,1)S(1)}, bf16[128,2176]{1,0:T(8,128)(2,1)S(1)}, u32[]{:S(2)}, u32[]{:S(2)}) %collective-permute-start.14) | collective-permute-done | bytes 557088 | tf_op jit(solution)/shard_map/ppermute | solution.py:480
  235.2 0.6 collective-permute-start.16
  235.9 1.1 collective-permute-start.15
  237.5 8.5 %collective-permute-done.16.refs_4_ = bf16[64,2176]{1,0:T(8,128)(2,1)} collective-permute-done((bf16[64,2176]{1,0:T(8,128)(2,1)S(1)}, bf16[64,2176]{1,0:T(8,128)(2,1)}, u32[]{:S(2)}, u32[]{:S(2)}) %collective-permute-start.16) | collective-permute-done | bytes 278560 | tf_op jit(solution)/shard_map/ppermute | solution.py:480
  245.9 1.0 collective-permute-done.15.refs_3_
  246.9 0.9 collective-permute-done.21.refs_9_
  247.8 1.0 collective-permute-done.20.refs_8_
  248.9 4.8 %shard_map.148 = bf16[4,64,2176]{2,1,0:T(8,128)(2,1)} custom-call(s32[1]{0:T(128)} %bitcast.14.row_ref, bf16[8,2,128,128]{3,2,1,0:T(8,128)(2,1)} %copy-done.5, bf16[128,2176]{1,0:T(8,128)(2,1)} %get-tuple-element.34.refs_0_, bf16[128,2176]{1,0:T(8,128)(2,1)} %copy-done.8, bf16[128,2176]{1,0:T(8,128)(2,1)} %copy-done.7, ...), custom_call_target="tpu_custom_call" | custom-call | flops 1073741824 | bytes 4194304 | tf_op jit(solution)/shard_map/pallas_call | solution.py:434
  253.6 8.0 %all-to-all-start.12 = ((bf16[4,64,2176]{2,1,0:T(8,128)(2,1)}), bf16[4,64,2176]{2,1,0:T(8,128)(2,1)S(1)}, u32[]{:S(2)}, u32[]{:S(2)}) async-start(bf16[4,64,2176]{2,1,0:T(8,128)(2,1)} %shard_map.148), calls=%async_computation.12 | async-start | bytes 2228224 | tf_op jit(solution)/shard_map/all_to_all | solution.py:530
  261.6 5.8 %shard_map.144 = bf16[16,128,128]{2,1,0:T(8,128)(2,1)} custom-call(bf16[16,128,128]{2,1,0:T(8,128)(2,1)} %copy-done, bf16[2048,4096]{1,0:T(8,128)(2,1)} %get-tuple-element.21.tile_ref), custom_call_target="tpu_custom_call" | custom-call | flops 2147483648 | bytes 8388608 | tf_op jit(solution)/shard_map/pallas_call | solution.py:232
  268.1 1.4 collective-permute-done.3.refs_0_
  269.5 0.8 copy-done.17
  270.3 6.5 %shard_map.145 = bf16[16,128,128]{2,1,0:T(8,128)(2,1)} custom-call(bf16[16,128,128]{2,1,0:T(8,128)(2,1)} %copy-done, bf16[2048,4096]{1,0:T(8,128)(2,1)} %get-tuple-element.21.tile_ref, bf16[16,128,128]{2,1,0:T(8,128)(2,1)} %copy-done.17), custom_call_target="tpu_custom_call" | custom-call | flops 2147483648 | bytes 8388608 | tf_op jit(solution)/shard_map/pallas_call | solution.py:232
  276.8 9.2 %all-to-all-done.12 = bf16[4,64,2176]{2,1,0:T(8,128)(2,1)S(1)} async-done(((bf16[4,64,2176]{2,1,0:T(8,128)(2,1)}), bf16[4,64,2176]{2,1,0:T(8,128)(2,1)S(1)}, u32[]{:S(2)}, u32[]{:S(2)}) %all-to-all-start.12) | async-done | bytes 1114144 | tf_op jit(solution)/shard_map/all_to_all | solution.py:530
  286.0 6.6 %all-to-all-start.8 = ((bf16[16,128,128]{2,1,0:T(8,128)(2,1)}), bf16[16,128,128]{2,1,0:T(8,128)(2,1)S(1)}, u32[]{:S(2)}, u32[]{:S(2)}) async-start(bf16[16,128,128]{2,1,0:T(8,128)(2,1)} %shard_map.145), calls=%async_computation.8 | async-start | bytes 1048576 | tf_op jit(solution)/shard_map/all_to_all | solution.py:483
  292.7 1.6 collective-permute-start.7
  294.5 1.6 collective-permute-start.6
  296.1 10.6 %collective-permute-done.7.refs_4_ = bf16[64,2176]{1,0:T(8,128)(2,1)S(1)} collective-permute-done((bf16[64,2176]{1,0:T(8,128)(2,1)S(1)}, bf16[64,2176]{1,0:T(8,128)(2,1)S(1)}, u32[]{:S(2)}, u32[]{:S(2)}) %collective-permute-start.7) | collective-permute-done | bytes 278560 | tf_op jit(solution)/shard_map/ppermute | solution.py:480
  307.3 1.0 collective-permute-done.12.refs_9_
  309.2 0.7 copy-done.23
  309.9 4.8 %shard_map.147 = bf16[4,64,2176]{2,1,0:T(8,128)(2,1)} custom-call(s32[1]{0:T(128)} %bitcast.14.row_ref, bf16[8,2,128,128]{3,2,1,0:T(8,128)(2,1)} %copy-done.4, bf16[128,2176]{1,0:T(8,128)(2,1)} %get-tuple-element.33.refs_0_, bf16[128,2176]{1,0:T(8,128)(2,1)} %copy-done.10, bf16[128,2176]{1,0:T(8,128)(2,1)} %copy-done.9, bf16[64,2176]{1,0:T(8,128)(2,1)} %copy-done.21, ...), custom_call_target="tpu_custom_call" | custom-call | flops 1073741824 | bytes 4194304 | tf_op jit(solution)/shard_map/pallas_call | solution.py:434
  314.7 4.3 %all-to-all-start.10 = ((bf16[4,64,2176]{2,1,0:T(8,128)(2,1)}), bf16[4,64,2176]{2,1,0:T(8,128)(2,1)S(1)}, u32[]{:S(2)}, u32[]{:S(2)}) async-start(bf16[4,64,2176]{2,1,0:T(8,128)(2,1)} %shard_map.147), calls=%async_computation.10 | async-start | bytes 2228224 | tf_op jit(solution)/shard_map/all_to_all | solution.py:530
  319.2 0.8 slice.73
  321.3 0.7 sqrt.8
  322.6 2.3 shard_map.146
  324.9 18.4 %all-to-all-done.10 = bf16[4,64,2176]{2,1,0:T(8,128)(2,1)S(1)} async-done(((bf16[4,64,2176]{2,1,0:T(8,128)(2,1)}), bf16[4,64,2176]{2,1,0:T(8,128)(2,1)S(1)}, u32[]{:S(2)}, u32[]{:S(2)}) %all-to-all-start.10) | async-done | bytes 1114144 | tf_op jit(solution)/shard_map/all_to_all | solution.py:530
  343.4 0.8 slice.68
  (97 shorter events, 6.0 us)
Async XLA Ops:
  0.6 5.5 %copy-start.3 = (bf16[128,2048]{1,0:T(8,128)(2,1)S(1)}, bf16[128,2048]{1,0:T(8,128)(2,1)}, u32[]{:S(2)}) copy-start(bf16[128,2048]{1,0:T(8,128)(2,1)} %input_ref.3) | copy-start | bytes 1572868
  2.4 8.7 %all-to-all-start = ((s32[4,32,256]{2,1,0:T(8,128)}), s32[4,32,256]{2,1,0:T(8,128)S(1)}, u32[]{:S(2)}, u32[]{:S(2)}) async-start(s32[4,32,256]{2,1,0:T(8,128)} %broadcast_in_dim.10), calls=%async_computation | async-start | bytes 262144 | tf_op jit(solution)/shard_map/all_to_all | solution.py:487
  11.1 17.9 %all-to-all-start.1 = ((bf16[128,16,128]{2,0,1:T(8,128)(2,1)}), bf16[128,16,128]{2,0,1:T(8,128)(2,1)S(1)}, u32[]{:S(2)}, u32[]{:S(2)}) async-start(bf16[128,16,128]{2,0,1:T(8,128)(2,1)} %copy_bitcast_fusion), calls=%async_computation.1 | async-start | bytes 1048576 | tf_op jit(solution)/shard_map/all_to_all | solution.py:504
  29.0 15.1 %copy-start.1 = (bf16[128,16,128]{2,0,1:T(8,128)(2,1)}, bf16[128,16,128]{2,0,1:T(8,128)(2,1)S(1)}, u32[]{:S(2)}) copy-start(bf16[128,16,128]{2,0,1:T(8,128)(2,1)S(1)} %all-to-all-done.1) | copy-start | bytes 1572868
  29.0 15.1 %collective-permute-start = (bf16[2048,128]{1,0:T(8,128)(2,1)S(1)}, bf16[2048,128]{1,0:T(8,128)(2,1)S(1)}, u32[]{:S(2)}, u32[]{:S(2)}) collective-permute-start(bf16[2048,128]{1,0:T(8,128)(2,1)S(1)} %bitcast.50), channel_id=1, source_target_pairs={{0,4},{4,0},{1,5},{5,1},{2,6},{6,2},{3,7},{7,3},{8,12},{12,8},{9,1... | collective-permute-start | bytes 1572872 | tf_op jit(solution)/shard_map/ppermute | solution.py:477
  44.1 0.8 copy-start.16
  44.9 17.9 %copy-start.24 = (s32[128]{0:T(128)S(1)}, s32[128]{0:T(128)}, u32[]{:S(2)}) copy-start(s32[128]{0:T(128)} %param.15) | copy-start | bytes 1540
  55.9 21.0 %all-to-all-start.2 = ((bf16[16,128,128]{2,1,0:T(8,128)(2,1)}), bf16[16,128,128]{2,1,0:T(8,128)(2,1)}, u32[]{:S(2)}, u32[]{:S(2)}) async-start(bf16[16,128,128]{2,1,0:T(8,128)(2,1)} %bitcast.57), calls=%async_computation.2 | async-start | bytes 1048576 | tf_op jit(solution)/shard_map/all_to_all | solution.py:483
  103.4 1.9 copy-start.2
  103.4 1.9 collective-permute-start.1
  105.3 0.8 copy-start.19
  117.1 21.0 %all-to-all-start.4 = ((bf16[16,128,128]{2,1,0:T(8,128)(2,1)}), bf16[16,128,128]{2,1,0:T(8,128)(2,1)}, u32[]{:S(2)}, u32[]{:S(2)}) async-start(bf16[16,128,128]{2,1,0:T(8,128)(2,1)} %bitcast.56), calls=%async_computation.4 | async-start | bytes 1048576 | tf_op jit(solution)/shard_map/all_to_all | solution.py:483
  177.5 3.5 %collective-permute-start.2 = (bf16[16,128,128]{2,1,0:T(8,128)(2,1)}, bf16[16,128,128]{2,1,0:T(8,128)(2,1)S(1)}, u32[]{:S(2)}, u32[]{:S(2)}) collective-permute-start(bf16[16,128,128]{2,1,0:T(8,128)(2,1)} %shard_map.141), channel_id=1, source_target_pairs={{0,4},{4,0},{1,5},{5,1},{2,6},{6,2},{3,7},{7,3},{8,12},{12,8},{9,1... | collective-permute-start | bytes 1572872 | tf_op jit(solution)/shard_map/ppermute | solution.py:477
  177.5 13.2 %all-to-all-start.9 = ((bf16[8,2,128,128]{3,2,1,0:T(8,128)(2,1)}), bf16[8,2,128,128]{3,2,1,0:T(8,128)(2,1)S(1)}, u32[]{:S(2)}, u32[]{:S(2)}) async-start(bf16[8,2,128,128]{3,2,1,0:T(8,128)(2,1)} %bitcast.15), calls=%async_computation.9 | async-start | bytes 1048576 | tf_op jit(solution)/shard_map/all_to_all | solution.py:515
  181.0 0.8 copy-start.18
  188.3 25.3 %copy-start.12 = (bf16[128,2176]{1,0:T(8,128)(2,1)S(1)}, bf16[128,2176]{1,0:T(8,128)(2,1)}, u32[]{:S(2)}) copy-start(bf16[128,2176]{1,0:T(8,128)(2,1)} %get-tuple-element.34.refs_0_) | copy-start | bytes 1671172
  190.7 33.5 %copy-start.4 = (bf16[8,2,128,128]{3,2,1,0:T(8,128)(2,1)}, bf16[8,2,128,128]{3,2,1,0:T(8,128)(2,1)S(1)}, u32[]{:S(2)}) copy-start(bf16[8,2,128,128]{3,2,1,0:T(8,128)(2,1)S(1)} %all-to-all-done.9.agg_ref) | copy-start | bytes 1572868
  210.0 14.2 %all-to-all-start.11 = ((bf16[8,2,128,128]{3,2,1,0:T(8,128)(2,1)}), bf16[8,2,128,128]{3,2,1,0:T(8,128)(2,1)S(1)}, u32[]{:S(2)}, u32[]{:S(2)}) async-start(bf16[8,2,128,128]{3,2,1,0:T(8,128)(2,1)} %bitcast.17), calls=%async_computation.11 | async-start | bytes 1048576 | tf_op jit(solution)/shard_map/all_to_all | solution.py:515
  213.5 21.6 %collective-permute-start.14 = (bf16[128,2176]{1,0:T(8,128)(2,1)S(1)}, bf16[128,2176]{1,0:T(8,128)(2,1)S(1)}, u32[]{:S(2)}, u32[]{:S(2)}) collective-permute-start(bf16[128,2176]{1,0:T(8,128)(2,1)S(1)} %copy-done.12), channel_id=1, source_target_pairs={{0,16},{8,24},{16,0},{24,8},{1,17},{9,25},{17,1},{25,9},{2,18},{10... | collective-permute-start | bytes 1671176 | tf_op jit(solution)/shard_map/ppermute | solution.py:480
  215.5 20.4 %collective-permute-start.13 = (bf16[128,2176]{1,0:T(8,128)(2,1)S(1)}, bf16[128,2176]{1,0:T(8,128)(2,1)S(1)}, u32[]{:S(2)}, u32[]{:S(2)}) collective-permute-start(bf16[128,2176]{1,0:T(8,128)(2,1)S(1)} %copy-done.12), channel_id=1, source_target_pairs={{0,8},{8,0},{16,24},{24,16},{1,9},{9,1},{17,25},{25,17},{2,10},{10... | collective-permute-start | bytes 1671176 | tf_op jit(solution)/shard_map/ppermute | solution.py:480
  224.2 24.6 %copy-start.5 = (bf16[8,2,128,128]{3,2,1,0:T(8,128)(2,1)}, bf16[8,2,128,128]{3,2,1,0:T(8,128)(2,1)S(1)}, u32[]{:S(2)}) copy-start(bf16[8,2,128,128]{3,2,1,0:T(8,128)(2,1)S(1)} %all-to-all-done.11.agg_ref) | copy-start | bytes 1572868
  224.2 29.4 %all-to-all-start.7 = ((bf16[16,128,128]{2,1,0:T(8,128)(2,1)}), bf16[16,128,128]{2,1,0:T(8,128)(2,1)S(1)}, u32[]{:S(2)}, u32[]{:S(2)}) async-start(bf16[16,128,128]{2,1,0:T(8,128)(2,1)} %get-tuple-element.31), calls=%async_computation.7 | async-start | bytes 1048576 | tf_op jit(solution)/shard_map/all_to_all | solution.py:483
  230.5 16.5 %collective-permute-start.17 = (bf16[128,2176]{1,0:T(8,128)(2,1)S(1)}, bf16[128,2176]{1,0:T(8,128)(2,1)S(1)}, u32[]{:S(2)}, u32[]{:S(2)}) collective-permute-start(bf16[128,2176]{1,0:T(8,128)(2,1)S(1)} %copy-done.12), channel_id=1, source_target_pairs={{0,4},{4,0},{1,5},{5,1},{2,6},{6,2},{3,7},{7,3},{8,12},{12,8},{9,1... | collective-permute-start | bytes 1671176 | tf_op jit(solution)/shard_map/ppermute | solution.py:477
  235.2 13.6 %copy-start.7 = (bf16[128,2176]{1,0:T(8,128)(2,1)}, bf16[128,2176]{1,0:T(8,128)(2,1)S(1)}, u32[]{:S(2)}) copy-start(bf16[128,2176]{1,0:T(8,128)(2,1)S(1)} %collective-permute-done.14.refs_2_) | copy-start | bytes 1671172
  235.2 10.7 %collective-permute-start.16 = (bf16[64,2176]{1,0:T(8,128)(2,1)S(1)}, bf16[64,2176]{1,0:T(8,128)(2,1)}, u32[]{:S(2)}, u32[]{:S(2)}) collective-permute-start(bf16[64,2176]{1,0:T(8,128)(2,1)S(1)} %slice.72), channel_id=1, source_target_pairs={{0,8},{8,0},{16,24},{24,16},{1,9},{9,1},{17,25},{25,17},{2,10},{10... | collective-permute-start | bytes 835592 | tf_op jit(solution)/shard_map/ppermute | solution.py:480
  235.8 13.0 %copy-start.8 = (bf16[128,2176]{1,0:T(8,128)(2,1)}, bf16[128,2176]{1,0:T(8,128)(2,1)S(1)}, u32[]{:S(2)}) copy-start(bf16[128,2176]{1,0:T(8,128)(2,1)S(1)} %collective-permute-done.13.refs_1_) | copy-start | bytes 1671172
  235.9 11.1 %collective-permute-start.15 = (bf16[64,2176]{1,0:T(8,128)(2,1)S(1)}, bf16[64,2176]{1,0:T(8,128)(2,1)}, u32[]{:S(2)}, u32[]{:S(2)}) collective-permute-start(bf16[64,2176]{1,0:T(8,128)(2,1)S(1)} %slice.71), channel_id=1, source_target_pairs={{0,16},{8,24},{16,0},{24,8},{1,17},{9,25},{17,1},{25,9},{2,18},{10... | collective-permute-start | bytes 835592 | tf_op jit(solution)/shard_map/ppermute | solution.py:480
  237.0 10.9 %collective-permute-start.19 = (bf16[128,2176]{1,0:T(8,128)(2,1)S(1)}, bf16[128,2176]{1,0:T(8,128)(2,1)}, u32[]{:S(2)}, u32[]{:S(2)}) collective-permute-start(bf16[128,2176]{1,0:T(8,128)(2,1)S(1)} %collective-permute-done.14.refs_2_), channel_id=1, source_target_pairs={{0,4},{4,0},{1,5},{5,1},{2,6},{6,2},{3,7},{7,3},{8,12},{12,8},{9,1... | collective-permute-start | bytes 1671176 | tf_op jit(solution)/shard_map/ppermute | solution.py:477
  237.0 11.9 %collective-permute-start.18 = (bf16[128,2176]{1,0:T(8,128)(2,1)S(1)}, bf16[128,2176]{1,0:T(8,128)(2,1)}, u32[]{:S(2)}, u32[]{:S(2)}) collective-permute-start(bf16[128,2176]{1,0:T(8,128)(2,1)S(1)} %collective-permute-done.13.refs_1_), channel_id=1, source_target_pairs={{0,4},{4,0},{1,5},{5,1},{2,6},{6,2},{3,7},{7,3},{8,12},{12,8},{9,1... | collective-permute-start | bytes 1671176 | tf_op jit(solution)/shard_map/ppermute | solution.py:477
  245.9 1.9 collective-permute-start.21
  246.9 1.9 collective-permute-start.20
  246.9 1.9 copy-start.13
  253.6 8.0 %copy-start = (bf16[16,128,128]{2,1,0:T(8,128)(2,1)}, bf16[16,128,128]{2,1,0:T(8,128)(2,1)S(1)}, u32[]{:S(2)}) copy-start(bf16[16,128,128]{2,1,0:T(8,128)(2,1)S(1)} %all-to-all-done.7.grad_ref) | copy-start | bytes 1572868
  253.6 32.4 %all-to-all-start.12 = ((bf16[4,64,2176]{2,1,0:T(8,128)(2,1)}), bf16[4,64,2176]{2,1,0:T(8,128)(2,1)S(1)}, u32[]{:S(2)}, u32[]{:S(2)}) async-start(bf16[4,64,2176]{2,1,0:T(8,128)(2,1)} %shard_map.148), calls=%async_computation.12 | async-start | bytes 2228224 | tf_op jit(solution)/shard_map/all_to_all | solution.py:530
  261.6 5.8 %copy-start.11 = (bf16[128,2176]{1,0:T(8,128)(2,1)S(1)}, bf16[128,2176]{1,0:T(8,128)(2,1)}, u32[]{:S(2)}) copy-start(bf16[128,2176]{1,0:T(8,128)(2,1)} %get-tuple-element.33.refs_0_) | copy-start | bytes 1671172
  267.4 2.1 collective-permute-start.3
  267.4 25.3 %collective-permute-start.5 = (bf16[128,2176]{1,0:T(8,128)(2,1)S(1)}, bf16[128,2176]{1,0:T(8,128)(2,1)S(1)}, u32[]{:S(2)}, u32[]{:S(2)}) collective-permute-start(bf16[128,2176]{1,0:T(8,128)(2,1)S(1)} %copy-done.11), channel_id=1, source_target_pairs={{0,16},{8,24},{16,0},{24,8},{1,17},{9,25},{17,1},{25,9},{2,18},{10... | collective-permute-start | bytes 1671176 | tf_op jit(solution)/shard_map/ppermute | solution.py:480
  267.8 26.7 %collective-permute-start.4 = (bf16[128,2176]{1,0:T(8,128)(2,1)S(1)}, bf16[128,2176]{1,0:T(8,128)(2,1)S(1)}, u32[]{:S(2)}, u32[]{:S(2)}) collective-permute-start(bf16[128,2176]{1,0:T(8,128)(2,1)S(1)} %copy-done.11), channel_id=1, source_target_pairs={{0,8},{8,0},{16,24},{24,16},{1,9},{9,1},{17,25},{25,17},{2,10},{10... | collective-permute-start | bytes 1671176 | tf_op jit(solution)/shard_map/ppermute | solution.py:480
  269.5 0.8 copy-start.17
  286.0 28.7 %all-to-all-start.8 = ((bf16[16,128,128]{2,1,0:T(8,128)(2,1)}), bf16[16,128,128]{2,1,0:T(8,128)(2,1)S(1)}, u32[]{:S(2)}, u32[]{:S(2)}) async-start(bf16[16,128,128]{2,1,0:T(8,128)(2,1)} %shard_map.145), calls=%async_computation.8 | async-start | bytes 1048576 | tf_op jit(solution)/shard_map/all_to_all | solution.py:483
  292.7 14.6 %collective-permute-start.8 = (bf16[128,2176]{1,0:T(8,128)(2,1)S(1)}, bf16[128,2176]{1,0:T(8,128)(2,1)S(1)}, u32[]{:S(2)}, u32[]{:S(2)}) collective-permute-start(bf16[128,2176]{1,0:T(8,128)(2,1)S(1)} %copy-done.11), channel_id=1, source_target_pairs={{0,4},{4,0},{1,5},{5,1},{2,6},{6,2},{3,7},{7,3},{8,12},{12,8},{9,1... | collective-permute-start | bytes 1671176 | tf_op jit(solution)/shard_map/ppermute | solution.py:477
  292.7 17.3 %copy-start.9 = (bf16[128,2176]{1,0:T(8,128)(2,1)}, bf16[128,2176]{1,0:T(8,128)(2,1)S(1)}, u32[]{:S(2)}) copy-start(bf16[128,2176]{1,0:T(8,128)(2,1)S(1)} %collective-permute-done.5.refs_2_) | copy-start | bytes 1671172
  292.7 14.0 %collective-permute-start.7 = (bf16[64,2176]{1,0:T(8,128)(2,1)S(1)}, bf16[64,2176]{1,0:T(8,128)(2,1)S(1)}, u32[]{:S(2)}, u32[]{:S(2)}) collective-permute-start(bf16[64,2176]{1,0:T(8,128)(2,1)S(1)} %slice.67), channel_id=1, source_target_pairs={{0,8},{8,0},{16,24},{24,16},{1,9},{9,1},{17,25},{25,17},{2,10},{10... | collective-permute-start | bytes 835592 | tf_op jit(solution)/shard_map/ppermute | solution.py:480
  294.3 14.0 %collective-permute-start.10 = (bf16[128,2176]{1,0:T(8,128)(2,1)S(1)}, bf16[128,2176]{1,0:T(8,128)(2,1)S(1)}, u32[]{:S(2)}, u32[]{:S(2)}) collective-permute-start(bf16[128,2176]{1,0:T(8,128)(2,1)S(1)} %collective-permute-done.5.refs_2_), channel_id=1, source_target_pairs={{0,4},{4,0},{1,5},{5,1},{2,6},{6,2},{3,7},{7,3},{8,12},{12,8},{9,1... | collective-permute-start | bytes 1671176 | tf_op jit(solution)/shard_map/ppermute | solution.py:477
  294.5 15.5 %copy-start.10 = (bf16[128,2176]{1,0:T(8,128)(2,1)}, bf16[128,2176]{1,0:T(8,128)(2,1)S(1)}, u32[]{:S(2)}) copy-start(bf16[128,2176]{1,0:T(8,128)(2,1)S(1)} %collective-permute-done.4.refs_1_) | copy-start | bytes 1671172
  294.5 12.7 %collective-permute-start.6 = (bf16[64,2176]{1,0:T(8,128)(2,1)S(1)}, bf16[64,2176]{1,0:T(8,128)(2,1)S(1)}, u32[]{:S(2)}, u32[]{:S(2)}) collective-permute-start(bf16[64,2176]{1,0:T(8,128)(2,1)S(1)} %slice.66), channel_id=1, source_target_pairs={{0,16},{8,24},{16,0},{24,8},{1,17},{9,25},{17,1},{25,9},{2,18},{10... | collective-permute-start | bytes 835592 | tf_op jit(solution)/shard_map/ppermute | solution.py:480
  296.1 13.9 %collective-permute-start.9 = (bf16[128,2176]{1,0:T(8,128)(2,1)S(1)}, bf16[128,2176]{1,0:T(8,128)(2,1)}, u32[]{:S(2)}, u32[]{:S(2)}) collective-permute-start(bf16[128,2176]{1,0:T(8,128)(2,1)S(1)} %collective-permute-done.4.refs_1_), channel_id=1, source_target_pairs={{0,4},{4,0},{1,5},{5,1},{2,6},{6,2},{3,7},{7,3},{8,12},{12,8},{9,1... | collective-permute-start | bytes 1671176 | tf_op jit(solution)/shard_map/ppermute | solution.py:477
  306.7 2.0 copy-start.20
  306.7 1.6 collective-permute-start.12
  307.2 1.6 copy-start.21
  307.2 1.6 collective-permute-start.11
  307.3 1.0 copy-start.14
  308.3 0.7 copy-start.22
  308.3 0.9 copy-start.15
  309.2 0.7 copy-start.23
  314.7 4.3 %copy-start.6 = (bf16[16,128,128]{2,1,0:T(8,128)(2,1)}, bf16[16,128,128]{2,1,0:T(8,128)(2,1)S(1)}, u32[]{:S(2)}) copy-start(bf16[16,128,128]{2,1,0:T(8,128)(2,1)S(1)} %all-to-all-done.8.up_ref) | copy-start | bytes 1572868
  314.7 28.5 %all-to-all-start.10 = ((bf16[4,64,2176]{2,1,0:T(8,128)(2,1)}), bf16[4,64,2176]{2,1,0:T(8,128)(2,1)S(1)}, u32[]{:S(2)}, u32[]{:S(2)}) async-start(bf16[4,64,2176]{2,1,0:T(8,128)(2,1)} %shard_map.147), calls=%async_computation.10 | async-start | bytes 2228224 | tf_op jit(solution)/shard_map/all_to_all | solution.py:530

commit v2 on v0

--- a/solution.py
+++ b/solution.py
@@ -1,7 +1,19 @@
+import functools
+
 import jax
 import jax.numpy as jnp
 from jax import lax
+from jax.experimental import pallas as pl
+from jax.experimental.pallas import tpu as pltpu
+from jax.sharding import Mesh
 from jax.sharding import PartitionSpec as P
+
+BF16, F32 = jnp.bfloat16, jnp.float32
+LANES = 128
+MXU = 256
+MIB = 1 << 20
+NT = (((1,), (1,)), ((), ()))
+GELU_C, GELU_A = 0.7978845608, 0.044715
 
 
 def gelu_value(value):
@@ -15,7 +27,7 @@
     return (live, block // col_devs, block % col_devs, safe % per_dev)
 
 
-def count_tile(lists, usable, local_index, span):
+def block_tile(lists, usable, local_index, span):
     columns = jnp.arange(span, dtype=jnp.int32)[None, :]
     marked = jnp.where(usable, local_index, -1)
     total = jnp.zeros((lists.shape[0], span), jnp.float32)
@@ -31,7 +43,7 @@
     )
 
 
-def local(features, weight_one, bias_one, weight_two, bias_two, cotangent, neighbours, valid_mask):
+def general(features, weight_one, bias_one, weight_two, bias_two, cotangent, neighbours, valid_mask):
     per_dev, width = features.shape
     row_devs = lax.axis_size("row")
     col_devs = lax.axis_size("col")
@@ -41,7 +53,7 @@
     scaling = inverse[:, None]
     validity = valid_mask.astype(jnp.float32)[:, None]
     live, src_row, src_col, offset = source_parts(neighbours, per_dev, col_devs)
-    front_tile = count_tile(
+    front_tile = block_tile(
         neighbours, live & (src_col == col_pos), src_row * per_dev + offset, row_devs * per_dev
     )
 
@@ -115,24 +127,732 @@
     )
 
 
+IN_VMEM = pl.BlockSpec(memory_space=pltpu.VMEM)
+IN_SMEM = pl.BlockSpec(memory_space=pltpu.SMEM)
+IN_ANY = pl.BlockSpec(memory_space=pl.ANY)
+COUNT = jnp.float8_e4m3fn
+PARAMS = pltpu.CompilerParams(vmem_limit_bytes=62 * MIB)
+
+
+def cost(flops, read, transcendentals=0):
+    return pl.CostEstimate(flops=flops, bytes_accessed=read, transcendentals=transcendentals)
+
+
+def lanes(at, size=LANES):
+    return slice(at * size, (at + 1) * size)
+
+
+def fetch(source, target, semaphore):
+    copy = pltpu.make_async_copy(source, target, semaphore)
+    copy.start()
+    return copy
+
+
+def stream(source, blocks, target, semaphores):
+    copies = [fetch(source.at[block], target.at[block], semaphores.at[i]) for i, block in enumerate(blocks)]
+
+    def arrivals():
+        for block, copy in zip(blocks, copies, strict=True):
+            copy.wait()
+            yield target[block]
+
+    return arrivals()
+
+
+def buffer(shape, blocks, dtype=BF16):
+    return [pltpu.VMEM(shape, dtype), pltpu.SemaphoreType.DMA((blocks,))]
+
+
+def like(value):
+    return [pltpu.VMEM(value.shape, value.dtype), pltpu.SemaphoreType.DMA]
+
+
+class Results:
+    def __init__(self, semaphores):
+        self.semaphores, self.copies = semaphores, []
+
+    def send(self, source, target):
+        self.copies.append(fetch(source, target, self.semaphores.at[len(self.copies)]))
+
+    def wait(self):
+        for copy in self.copies:
+            copy.wait()
+
+
+def column_blocks(size, step):
+    return [(slice(None), slice(at, at + step)) for at in range(0, size, step)]
+
+
+def row_blocks(size, step):
+    return [(slice(at, at + step), slice(None)) for at in range(0, size, step)]
+
+
+def tile_kernel(turn, nodes, cols, place_ref, lists_ref, tile_ref):
+    masks, lines, width = lists_ref.shape
+    groups = 8
+    rows = LANES // groups
+    chip_row, core = place_ref[0] // 2, place_ref[0] % 2
+    step = pl.program_id(0)
+    per_chip = lines // groups
+    mask = chip_row ^ (step // per_chip)
+    lists = lists_ref[mask, pl.ds(pl.multiple_of(step % per_chip * groups, groups), groups), :]
+    node_bits, col_bits = nodes.bit_length() - 1, cols.bit_length() - 1
+    owner_row = lists >> (node_bits + col_bits)
+    within = lists & (nodes * cols - 1)
+    place = ((owner_row >> 1) << (node_bits + col_bits)) + within
+    live = lists >= 0
+    if turn:
+        half = masks * cols * nodes
+        place = jnp.where((owner_row & 1) == core, place, place + half)
+    else:
+        live &= (owner_row & 1) == core
+    line = lax.broadcasted_iota(jnp.int32, lists.shape, 1) // rows
+    highs = jnp.where(live, (place // MXU) * rows + line, -1)
+    lows = place % MXU
+    blocks = (tile_ref.shape[0] if turn else tile_ref.shape[1]) // MXU
+    high_place = lax.broadcasted_iota(jnp.int32, (blocks * rows, width), 0)
+    low_place = lax.broadcasted_iota(jnp.int32, (MXU, width), 0)
+    pieces = []
+    for group in range(groups):
+        high = (high_place == highs[group : group + 1, :]).astype(F32).astype(BF16)
+        low = (low_place == lows[group : group + 1, :]).astype(F32).astype(BF16)
+        counts = lax.dot_general(high, low, NT, preferred_element_type=F32)
+        pieces.append(counts.astype(BF16))
+    for block in range(blocks):
+        column = jnp.concatenate([piece[block * rows : (block + 1) * rows] for piece in pieces], axis=0)
+        if turn:
+            for side in range(2):
+                turned = column[:, lanes(side)].T
+                tile_ref[lanes(2 * block + side), :] = turned.astype(COUNT)
+        else:
+            tile_ref[:, lanes(block, MXU)] = column.astype(COUNT)
+
+
+def count_tile(at, lists, nodes, cols, turn):
+    masks, lines, width = lists.shape
+    rows = masks * lines * 16
+    half = masks * cols * nodes
+    shape = (2 * half, rows) if turn else (rows, half)
+    block = (2 * half, LANES) if turn else (LANES, half)
+    return pl.pallas_call(
+        functools.partial(tile_kernel, turn, nodes, cols),
+        grid=(rows // LANES,),
+        in_specs=[IN_SMEM, pl.BlockSpec(lists.shape, lambda i: (0, 0, 0))],
+        out_specs=pl.BlockSpec(block, (lambda i: (0, i)) if turn else (lambda i: (i, 0))),
+        out_shape=jax.ShapeDtypeStruct(shape, COUNT),
+        compiler_params=PARAMS,
+        cost_estimate=cost(4 * rows * shape[0 if turn else 1] * 2 * MXU, rows * half),
+    )(at, lists)
+
+
+def adjacency_kernel(forward, tiles, own_ref, other_ref, *refs):
+    tile_refs, refs = refs[:tiles], refs[-10 - tiles :]
+    out_ref, left_ref, total_ref, own, own_sem, other, other_sem = refs[:7]
+    buffers, (semaphores, out, out_sems) = refs[7 : 7 + tiles], refs[7 + tiles :]
+    chips, width = own_ref.shape[0], LANES
+    half = chips * width
+    copies = [fetch(own_ref, own, own_sem), fetch(other_ref, other, other_sem)]
+    chunks, arrivals = [], []
+    for ref, target in zip(tile_refs, buffers, strict=True):
+        for at in range(0, ref.shape[0], half):
+            here = slice(at, at + half)
+            arrivals.append(fetch(ref.at[here], target.at[here], semaphores.at[len(chunks)]))
+            chunks.append(target.at[here])
+    for copy in copies:
+        copy.wait()
+    for at in range(chips):
+        left_ref[:width, lanes(at)] = own[at].T if forward else own[at]
+        left_ref[:width, lanes(chips + at)] = other[at].T if forward else other[at]
+    if forward:
+        left_ref[width:, :] = jnp.ones((left_ref.shape[0] - width, left_ref.shape[1]), BF16)
+    for block, (copy, counts) in enumerate(zip(arrivals, chunks, strict=True)):
+        copy.wait()
+        part = jnp.dot(left_ref[:, lanes(block, half)], counts[...].astype(BF16), preferred_element_type=F32)
+        if block == 0:
+            total_ref[...] = part
+        else:
+            total_ref[...] += part
+    results = Results(out_sems)
+    group = chips // out_sems.shape[0]
+    for at in range(chips):
+        here = lanes(at)
+        if forward:
+            inverse = 1.0 / (total_ref[width : width + 1, here] + 1.0)
+            value = (total_ref[:width, here] + 2.0 * left_ref[:width, here].astype(F32)) * inverse
+            out[at] = value.astype(BF16).T
+        else:
+            out[at] = total_ref[:, here].astype(BF16)
+        if (at + 1) % group == 0:
+            done = slice(at + 1 - group, at + 1)
+            results.send(out.at[done], out_ref.at[done])
+    results.wait()
+
+
+def apply_adjacency(tiles, own, other, forward, *after):
+    sources, half = sum(tile.shape[0] for tile in tiles), tiles[0].shape[1]
+    rows = LANES + (16 if forward else 0)
+    scratch = [pltpu.VMEM((rows, sources), BF16), pltpu.VMEM((rows, half), F32)] + like(own) + like(other)
+    scratch += [pltpu.VMEM(tile.shape, COUNT) for tile in tiles] + [pltpu.SemaphoreType.DMA((sources // half,))]
+    return pl.pallas_call(
+        functools.partial(adjacency_kernel, forward, len(tiles)),
+        in_specs=[IN_ANY] * (2 + len(tiles) + len(after)),
+        out_specs=IN_ANY,
+        out_shape=jax.ShapeDtypeStruct(own.shape, BF16),
+        scratch_shapes=scratch + buffer(own.shape, 4),
+        compiler_params=PARAMS,
+        cost_estimate=cost(2 * half * sources * LANES, half * sources),
+    )(own, other, *tiles, *after)
+
+
+def gelu_parts(pre, valid):
+    square = pre * pre
+    bend = jnp.tanh(GELU_C * (pre + GELU_A * (square * pre)))
+    inner = GELU_C * (1.0 + 3.0 * GELU_A * square)
+    slope = 0.5 * (1.0 + bend) + 0.5 * pre * (1.0 - bend * bend) * inner
+    return valid * (0.5 * pre * (1.0 + bend)), valid * slope
+
+
+def lane_squares(value, valid):
+    value = value.astype(F32)
+    value = jnp.sum(valid * (value * value), axis=0, keepdims=True)
+    return sum(value[:, lanes(i)] for i in range(value.shape[1] // LANES))
+
+
+def send_pieces(at_ref, agg_blocks, pieces, piece_refs, results):
+    chip_row = at_ref[0] // 2
+    blocks = agg_blocks.shape[0] // len(piece_refs)
+    for mask, ref in enumerate(piece_refs):
+        for part in range(blocks):
+            pieces[mask, :, lanes(part)] = agg_blocks[(chip_row ^ mask) * blocks + part]
+        results.send(pieces.at[mask], ref)
+
+
+def first_kernel(at_ref, agg_ref, weight_ref, bias_ref, valid_ref, input_ref, *refs):
+    out_ref, slope_ref, stat_ref = refs[-17:-14]
+    piece_refs = refs[-14:-10]
+    agg_blocks, agg_sem, inputs, input_sem, weight_buffer, semaphores = refs[-10:-4]
+    out, slopes, pieces, out_sems = refs[-4:]
+    chips, nodes, width = agg_ref.shape
+    full = weight_ref.shape[1]
+    step = full // semaphores.shape[0]
+    copies = [fetch(agg_ref, agg_blocks, agg_sem)]
+    weights = stream(weight_ref, column_blocks(full, step), weight_buffer, semaphores)
+    copies.append(fetch(input_ref, inputs, input_sem))
+    results = Results(out_sems)
+    valid = valid_ref[...]
+    copies[0].wait()
+    agg = jnp.concatenate([agg_blocks[i] for i in range(chips)], axis=1)
+    send_pieces(at_ref, agg_blocks, pieces, piece_refs, results)
+    none = jnp.zeros((1, LANES), F32)
+    of_agg, of_input, of_out, of_low = lane_squares(agg, valid), none, none, none
+    for block, weight in enumerate(weights):
+        here = lanes(block, step)
+        pre = jnp.dot(agg, weight, preferred_element_type=F32) + bias_ref[:, here]
+        value, slopes[:, here] = gelu_parts(pre, valid)
+        low = value.astype(BF16)
+        of_out += lane_squares(value, valid)
+        of_low += lane_squares(low, valid)
+        if block == 0:
+            copies[1].wait()
+        of_input += lane_squares(inputs[:, here], valid)
+        blocks = lanes(block, step // LANES)
+        for part in range(step // LANES):
+            out[blocks.start + part] = low[:, lanes(part)]
+        results.send(out.at[blocks], out_ref.at[blocks])
+        results.send(slopes.at[:, here], slope_ref.at[:, here])
+    count = jnp.sum(jnp.broadcast_to(valid, (nodes, LANES)), axis=0, keepdims=True) * (1.0 / LANES)
+    stat_ref[...] = jnp.concatenate([of_input, of_agg, of_out, of_low, count, none, none, none], axis=0)
+    results.wait()
+
+
+def piece_shapes(agg, chip_rows):
+    chips, nodes, width = agg.shape
+    return [jax.ShapeDtypeStruct((nodes, chips * width // chip_rows), BF16)] * chip_rows
+
+
+def first_layer(at, agg, weight, bias, valid, inputs, chip_rows, *after):
+    chips, nodes, width = agg.shape
+    full = weight.shape[1]
+    pieces = piece_shapes(agg, chip_rows)
+    steps = 2
+    return pl.pallas_call(
+        first_kernel,
+        in_specs=[IN_SMEM, IN_ANY, IN_ANY, IN_VMEM, IN_VMEM, IN_ANY] + [IN_ANY] * len(after),
+        out_specs=[IN_ANY, IN_ANY, IN_VMEM] + [IN_ANY] * chip_rows,
+        out_shape=[
+            jax.ShapeDtypeStruct(agg.shape, BF16),
+            jax.ShapeDtypeStruct((nodes, full), F32),
+            jax.ShapeDtypeStruct((8, LANES), F32),
+        ]
+        + pieces,
+        scratch_shapes=like(agg)
+        + like(inputs)
+        + buffer(weight.shape, steps)
+        + [
+            pltpu.VMEM(agg.shape, BF16),
+            pltpu.VMEM((nodes, full), F32),
+            pltpu.VMEM((chip_rows,) + pieces[0].shape, BF16),
+            pltpu.SemaphoreType.DMA((chip_rows + 2 * steps,)),
+        ],
+        compiler_params=PARAMS,
+        cost_estimate=cost(2 * nodes * full * full, 2 * full * full, nodes * full),
+    )(at, agg, weight, bias, valid, inputs, *after)
+
+
+def gradient_blocks(weight, blocks, turned, inverse, outs, refs, results):
+    low = jnp.dot(weight, turned[...], preferred_element_type=F32).astype(BF16)
+    sums = (low.astype(F32) * inverse).astype(BF16)
+    for value, out, ref in zip((sums, low), outs, refs, strict=True):
+        for part in range(weight.shape[0] // LANES):
+            out[blocks.start + part] = value[lanes(part)]
+        results.send(out.at[blocks], ref.at[blocks])
+
+
+def second_kernel(
+    at_ref, agg_ref, weight_ref, bias_ref, valid_ref, cotangent_ref, inverse_ref, stat_ref, *refs
+):
+    act_ref, pre_ref, sums_ref, grad_agg_ref = refs[-21:-17]
+    piece_refs = refs[-17:-13]
+    agg_blocks, agg_sem, cotangent, cotangent_sem, weight_buffer, semaphores = refs[-13:-7]
+    act, pres, turned, sums, grad_agg, pieces, out_sems = refs[-7:]
+    chips, nodes, width = agg_ref.shape
+    full = weight_ref.shape[1]
+    step = full // semaphores.shape[0]
+    copies = [fetch(agg_ref, agg_blocks, agg_sem)]
+    weights = stream(weight_ref, column_blocks(full, step), weight_buffer, semaphores)
+    copies.append(fetch(cotangent_ref, cotangent, cotangent_sem))
+    results = Results(out_sems)
+    valid, inverse = valid_ref[...], inverse_ref[...]
+    copies[0].wait()
+    agg = jnp.concatenate([agg_blocks[i] for i in range(chips)], axis=1)
+    send_pieces(at_ref, agg_blocks, pieces, piece_refs, results)
+    of_agg, of_out = lane_squares(agg, valid), jnp.zeros((1, LANES), F32)
+    for block, weight in enumerate(weights):
+        here = lanes(block, step)
+        pre = jnp.dot(agg, weight, preferred_element_type=F32) + bias_ref[:, here]
+        value, slope = gelu_parts(pre, valid)
+        of_out += lane_squares(value, valid)
+        act[:, here] = value.astype(BF16)
+        results.send(act.at[:, here], act_ref.at[:, here])
+        if block == 0:
+            copies[1].wait()
+        grad_pre = (cotangent[:, here].astype(F32) * slope).astype(BF16)
+        pres[:, here] = grad_pre
+        for part in range(step // LANES):
+            turned[block * step + part * LANES : block * step + (part + 1) * LANES, :] = grad_pre[:, lanes(part)].T
+    stat = stat_ref[...]
+    rows = [stat[:4], of_agg, of_out, stat[4:5], jnp.zeros((1, LANES), F32)]
+    total = jnp.sum(jnp.concatenate(rows, axis=0), axis=1, keepdims=True)
+    high = total.astype(BF16).astype(F32)
+    both = jnp.concatenate([high, total - high], axis=0)
+    pres[:16, full:] = jnp.broadcast_to(both, (16, LANES)).astype(BF16)
+    pres[16:, full:] = jnp.zeros((nodes - 16, LANES), BF16)
+    results.send(pres, pre_ref)
+    step = full // 4
+    for block in range(4):
+        gradient_blocks(
+            weight_buffer[lanes(block, step), :], lanes(block, step // LANES), turned, inverse,
+            (sums, grad_agg), (sums_ref, grad_agg_ref), results,
+        )
+    results.wait()
+
+
+def second_layer(at, agg, weight, bias, valid, cotangent, inverse, stats, chip_rows, *after):
+    chips, nodes, width = agg.shape
+    full = weight.shape[1]
+    blocks = jax.ShapeDtypeStruct((chips, width, nodes), BF16)
+    pieces = piece_shapes(agg, chip_rows)
+    steps = 2
+    return pl.pallas_call(
+        second_kernel,
+        in_specs=[IN_SMEM, IN_ANY, IN_ANY, IN_VMEM, IN_VMEM, IN_ANY, IN_VMEM, IN_VMEM] + [IN_ANY] * len(after),
+        out_specs=[IN_ANY] * (4 + chip_rows),
+        out_shape=[
+            jax.ShapeDtypeStruct((nodes, full), BF16),
+            jax.ShapeDtypeStruct((nodes, full + LANES), BF16),
+            blocks,
+            blocks,
+        ]
+        + pieces,
+        scratch_shapes=like(agg)
+        + like(cotangent)
+        + buffer(weight.shape, steps)
+        + [
+            pltpu.VMEM((nodes, full), BF16),
+            pltpu.VMEM((nodes, full + LANES), BF16),
+            pltpu.VMEM((full, nodes), BF16),
+            pltpu.VMEM(blocks.shape, BF16),
+            pltpu.VMEM(blocks.shape, BF16),
+            pltpu.VMEM((chip_rows,) + pieces[0].shape, BF16),
+            pltpu.SemaphoreType.DMA((chip_rows + steps + 1 + 8,)),
+        ],
+        compiler_params=PARAMS,
+        cost_estimate=cost(4 * nodes * full * full, 2 * full * full, nodes * full),
+    )(at, agg, weight, bias, valid, cotangent, inverse, stats, *after)
+
+
+def back_kernel(slope_ref, weight_ref, inverse_ref, up_ref, extra_ref, *refs):
+    pre_ref, sums_ref, agg_ref, slope, slope_sem, up, up_sem, extra, extra_sem = refs[-16:-7]
+    weight_buffer, semaphores, pres, turned, sums, grad_agg, out_sems = refs[-7:]
+    nodes, full = slope_ref.shape
+    step = full // semaphores.shape[0]
+    copies = [fetch(up_ref, up, up_sem), fetch(extra_ref, extra, extra_sem), fetch(slope_ref, slope, slope_sem)]
+    weights = stream(weight_ref, row_blocks(full, step), weight_buffer, semaphores)
+    results = Results(out_sems)
+    inverse = inverse_ref[...]
+    for copy in copies:
+        copy.wait()
+    for at in range(up_ref.shape[0]):
+        value = up[at].astype(F32) + 2.0 * extra[at].astype(F32) * inverse
+        grad_pre = (value.T * slope[:, lanes(at)]).astype(BF16)
+        pres[:, lanes(at)] = grad_pre
+        turned[lanes(at), :] = grad_pre.T
+    pres[:, full:] = jnp.zeros((nodes, LANES), BF16)
+    results.send(pres, pre_ref)
+    for block, weight in enumerate(weights):
+        gradient_blocks(
+            weight, lanes(block, step // LANES), turned, inverse, (sums, grad_agg), (sums_ref, agg_ref), results
+        )
+    results.wait()
+
+
+def first_layer_back(slope, weight, inverse, upstream, extra, *after):
+    nodes, full = slope.shape
+    blocks = jax.ShapeDtypeStruct(upstream.shape, BF16)
+    steps = 1
+    return pl.pallas_call(
+        back_kernel,
+        in_specs=[IN_ANY, IN_ANY, IN_VMEM, IN_ANY, IN_ANY] + [IN_ANY] * len(after),
+        out_specs=[IN_ANY] * 3,
+        out_shape=[jax.ShapeDtypeStruct((nodes, full + LANES), BF16), blocks, blocks],
+        scratch_shapes=like(slope)
+        + like(upstream)
+        + like(extra)
+        + buffer(weight.shape, steps)
+        + [
+            pltpu.VMEM((nodes, full + LANES), BF16),
+            pltpu.VMEM((full, nodes), BF16),
+            pltpu.VMEM(blocks.shape, BF16),
+            pltpu.VMEM(blocks.shape, BF16),
+            pltpu.SemaphoreType.DMA((1 + 2 * steps,)),
+        ],
+        compiler_params=PARAMS,
+        cost_estimate=cost(2 * nodes * full * full, 2 * full * full),
+    )(slope, weight, inverse, upstream, extra, *after)
+
+
+def left_factor(at_ref, lefts, left_parts, left_sem, left_ref):
+    nodes = lefts[0].shape[0]
+    width = left_parts.shape[2]
+    mine = pl.ds(pl.multiple_of(at_ref[0] % 2 * width, width), width)
+    copies = [fetch(ref.at[:, mine], left_parts.at[i], left_sem.at[i]) for i, ref in enumerate(lefts)]
+
+    def finish():
+        for i, copy in enumerate(copies):
+            copy.wait()
+            left_ref[:width, lanes(i, nodes)] = left_parts[i].T
+        left_ref[width:, :] = jnp.ones((left_ref.shape[0] - width, left_ref.shape[1]), BF16)
+
+    return finish
+
+
+def products(at_ref, left_ref, right, copies, width, use):
+    bias = jnp.zeros((8, width), F32)
+    step = right.shape[1] // len(copies)
+    for block, group in enumerate(copies):
+        for copy in group:
+            copy.wait()
+        here = lanes(block, step)
+        total = jnp.dot(left_ref[...], right[:, here], preferred_element_type=F32)
+        use(here, total)
+        for part in range(step // width):
+            one = block * (step // width) + part
+            bias += jnp.where(at_ref[0] == one, total[width : width + 8, lanes(part, width)], 0.0)
+    return bias
+
+
+def second_weight_kernel(at_ref, *refs):
+    lefts, right_ref = refs[:8], refs[8]
+    out_ref, side_ref, left_parts, left_sem, right, right_sems, stat_parts, stat_sems, left_ref = refs[-9:]
+    nodes, width = left_parts.shape[1:]
+    full = right.shape[1]
+    finish = left_factor(at_ref, lefts, left_parts, left_sem, left_ref)
+    rows = [pl.ds(pl.multiple_of((at_ref[0] ^ i) * nodes, nodes), nodes) for i in range(8)]
+    steps = right_sems.shape[0]
+    copies = [
+        [
+            fetch(
+                right_ref.at[source, lanes(block, full // steps)],
+                right.at[lanes(i, nodes), lanes(block, full // steps)],
+                right_sems.at[block, i],
+            )
+            for i, source in enumerate(rows)
+        ]
+        for block in range(steps)
+    ]
+    stat_copies = [
+        fetch(right_ref.at[lanes(i, nodes), slice(full, full + LANES)], stat_parts.at[i], stat_sems.at[i])
+        for i in range(8)
+    ]
+    finish()
+
+    def use(here, total):
+        out_ref[:, here] = total[:width].astype(BF16)
+
+    side_ref[:8, :] = products(at_ref, left_ref, right, copies, width, use)
+    stats = jnp.zeros((8, LANES), F32)
+    for i, copy in enumerate(stat_copies):
+        copy.wait()
+        both = stat_parts[i, :16].astype(F32)
+        stats += both[:8] + both[8:]
+    side_ref[8:, :LANES] = stats
+    side_ref[8:, LANES:] = jnp.zeros((8, width - LANES), F32)
+
+
+def second_weight(at, lefts, right):
+    rows, full = right.shape
+    full -= LANES
+    nodes, width = rows // 8, lefts[0].shape[1] // 2
+    return pl.pallas_call(
+        second_weight_kernel,
+        in_specs=[IN_SMEM] + [IN_ANY] * 9,
+        out_specs=[IN_VMEM] * 2,
+        out_shape=[jax.ShapeDtypeStruct((width, full), BF16), jax.ShapeDtypeStruct((16, width), F32)],
+        scratch_shapes=[
+            pltpu.VMEM((8, nodes, width), BF16),
+            pltpu.SemaphoreType.DMA((8,)),
+            pltpu.VMEM((rows, full), BF16),
+            pltpu.SemaphoreType.DMA((2, 8)),
+            pltpu.VMEM((8, nodes, LANES), BF16),
+            pltpu.SemaphoreType.DMA((8,)),
+            pltpu.VMEM((width + 16, rows), BF16),
+        ],
+        compiler_params=PARAMS,
+        cost_estimate=cost(2 * rows * full * width, 4 * rows * full),
+    )(at, *lefts, right)
+
+
+def first_weight_kernel(at_ref, side_ref, *refs):
+    lefts, rights, outs = refs[:8], refs[8:-9], refs[-9:-5]
+    left_parts, left_sem, right, right_sems, left_ref = refs[-5:]
+    col = at_ref[1]
+    piece_rows, full = outs[0].shape
+    full -= LANES
+    nodes, width = left_parts.shape[1:]
+    finish = left_factor(at_ref, lefts, left_parts, left_sem, left_ref)
+    steps = right_sems.shape[0]
+    starts = [sum(ref.shape[0] for ref in rights[:i]) for i in range(len(rights))]
+    copies = [
+        [
+            fetch(
+                ref.at[:, lanes(block, full // steps)],
+                right.at[slice(start, start + ref.shape[0]), lanes(block, full // steps)],
+                right_sems.at[block, i],
+            )
+            for i, (ref, start) in enumerate(zip(rights, starts, strict=True))
+        ]
+        for block in range(steps)
+    ]
+    finish()
+
+    def use(here, total):
+        for mask, ref in enumerate(outs):
+            value = total[:piece_rows]
+            for piece in range(1, len(outs)):
+                value = jnp.where(col ^ mask == piece, total[piece * piece_rows : (piece + 1) * piece_rows], value)
+            ref[:, here] = value.astype(BF16)
+
+    bias_one = products(at_ref, left_ref, right, copies, width, use)
+    bias_two, stats = side_ref[:8, :], side_ref[8:, :LANES]
+    stats_high = stats.astype(BF16).astype(F32)
+    rest = jnp.zeros((piece_rows - 24, LANES), F32)
+    line = lax.broadcasted_iota(jnp.int32, (8, LANES), 0)
+    for mask, ref in enumerate(outs):
+        piece = col ^ mask
+        rows = []
+        for bias in (bias_one, bias_two):
+            one = jnp.where(piece >= 2, bias[:, LANES:], bias[:, :LANES])
+            one = jnp.where(piece % 2 == 1, pltpu.roll(one, LANES // 2, 1), one)
+            high = one.astype(BF16).astype(F32)
+            rows += [high, one - high]
+        first = jnp.zeros((8, LANES), F32)
+        for i, row in enumerate(rows):
+            first = jnp.where(line == i, row, first)
+        ref[:, full:] = jnp.concatenate([first, stats_high, stats - stats_high, rest], axis=0).astype(BF16)
+
+
+def first_weight(at, side, lefts, rights, cols):
+    nodes, full = lefts[0].shape[0], rights[0].shape[1]
+    full -= LANES
+    width = lefts[0].shape[1] // 2
+    return pl.pallas_call(
+        first_weight_kernel,
+        in_specs=[IN_SMEM, IN_VMEM] + [IN_ANY] * (8 + len(rights)),
+        out_specs=[IN_VMEM] * cols,
+        out_shape=[jax.ShapeDtypeStruct((width // cols, full + LANES), BF16)] * cols,
+        scratch_shapes=[
+            pltpu.VMEM((8, nodes, width), BF16),
+            pltpu.SemaphoreType.DMA((8,)),
+            pltpu.VMEM((8 * nodes, full), BF16),
+            pltpu.SemaphoreType.DMA((2, len(rights))),
+            pltpu.VMEM((width + 16, 8 * nodes), BF16),
+        ],
+        compiler_params=PARAMS,
+        cost_estimate=cost(2 * 8 * nodes * full * width, 4 * 8 * nodes * full),
+    )(at, side, *lefts, *rights)
+
+
+def sum_kernel(*refs):
+    parts, (out_ref, bias_ref, stat_ref) = refs[:-3], refs[-3:]
+    full = out_ref.shape[1]
+    step = 512
+    for at in range(0, full, step):
+        here = slice(at, at + step)
+        out_ref[:, here] = sum([part[:, here].astype(F32) for part in parts[1:]], parts[0][:, here].astype(F32))
+    extra = sum([part[:, full:].astype(F32) for part in parts[1:]], parts[0][:, full:].astype(F32))
+    bias_ref[0:1, :] = extra[0:1] + extra[1:2]
+    bias_ref[1:2, :] = extra[2:3] + extra[3:4]
+    stat_ref[...] = extra[8:16] + extra[16:24]
+
+
+def sum_pieces(parts):
+    rows, full = parts[0].shape
+    full -= LANES
+    return pl.pallas_call(
+        sum_kernel,
+        in_specs=[IN_VMEM] * len(parts),
+        out_specs=[IN_VMEM] * 3,
+        out_shape=[
+            jax.ShapeDtypeStruct((rows, full), F32),
+            jax.ShapeDtypeStruct((2, LANES), F32),
+            jax.ShapeDtypeStruct((8, LANES), F32),
+        ],
+        compiler_params=PARAMS,
+    )(*parts)
+
+
+def final_kernel(up_ref, agg_ref, inverse_ref, out_ref):
+    inverse = inverse_ref[...]
+    for at in range(up_ref.shape[0]):
+        value = up_ref[at].astype(F32) + 2.0 * agg_ref[at].astype(F32) * inverse
+        out_ref[:, lanes(at)] = value.T.astype(BF16)
+
+
+def input_gradient(upstream, grad_agg, inverse):
+    chips, width, nodes = upstream.shape
+    return pl.pallas_call(
+        final_kernel,
+        in_specs=[IN_VMEM] * 3,
+        out_specs=IN_VMEM,
+        out_shape=jax.ShapeDtypeStruct((nodes, chips * width), BF16),
+        compiler_params=PARAMS,
+    )(upstream, grad_agg, inverse)
+
+
+def transposed(features, weight_one, bias_one, weight_two, bias_two, cotangent, neighbours, valid_mask):
+    nodes, full = features.shape
+    chip_rows, cols = lax.axis_size("ch"), lax.axis_size("col")
+    chips = chip_rows * cols
+    core = lax.axis_index("core")
+    col = lax.axis_index("col")
+    row = (2 * lax.axis_index("ch") + core).reshape(1)
+    every = ("ch", "col")
+
+    def swap(value):
+        return lax.ppermute(value, "core", [(0, 1), (1, 0)])
+
+    def across(value, mask):
+        return lax.ppermute(value, "ch", [(i, i ^ mask) for i in range(chip_rows)])
+
+    def exchange(value):
+        return lax.all_to_all(value, every, 0, 0, tiled=True)
+
+    at = jnp.concatenate([row, col.reshape(1)])
+
+    lists = neighbours.reshape(-1, MXU)
+    lists = jnp.stack([lists] + [across(lists, mask) for mask in range(1, chip_rows)])
+    own = exchange(jnp.transpose(features.reshape(nodes, chips, LANES), (1, 0, 2)))
+    turned = count_tile(at, lists, nodes, cols, True)
+    tile_own = count_tile(at, lists, nodes, cols, False)
+    tile_other = count_tile(at, swap(lists), nodes, cols, False)
+
+    own_lists = lax.dynamic_slice_in_dim(neighbours, col * nodes, nodes, 0)
+    inverse = 1.0 / (jnp.sum(own_lists >= 0, axis=1).astype(F32) + 1.0)
+    inverse = inverse.reshape(1, nodes)
+    valid = valid_mask.astype(F32).reshape(nodes, 1)
+
+    def to_plane(parts):
+        return [parts[0]] + [across(parts[mask], mask) for mask in range(1, chip_rows)]
+
+    def both_cores(parts):
+        return [part for one in parts for part in (one, swap(one))]
+
+    def over_cols(parts):
+        return [parts[0]] + [
+            lax.ppermute(parts[mask], "col", [(i, i ^ mask) for i in range(cols)]) for mask in range(1, cols)
+        ]
+
+    def exchange_beside(value, *others):
+        return lax.optimization_barrier((exchange(value), *others))
+
+    own, turned = lax.optimization_barrier((own, turned))
+    agg_one = exchange(apply_adjacency([turned], own, swap(own), True))
+    agg_one, tile_own = lax.optimization_barrier((agg_one, tile_own))
+    hidden, slope_one, stats_one, *pieces_one = first_layer(
+        at, agg_one, weight_one, bias_one.reshape(1, -1), valid, features, chip_rows
+    )
+    own, tile_other = exchange_beside(hidden, tile_other)
+    agg_two = apply_adjacency([turned], own, swap(own), True)
+    agg_two, *pieces_one = exchange_beside(agg_two, *to_plane(pieces_one))
+    act, grad_pre_two, sums_two, grad_agg_two, *pieces_two = second_layer(
+        at, agg_two, weight_two, bias_two.reshape(1, -1), valid, cotangent, inverse, stats_one, chip_rows
+    )
+    all_two = lax.all_gather(grad_pre_two, ("ch", "core"), axis=0, tiled=True)
+    own, *pieces_two = exchange_beside(sums_two, *to_plane(pieces_two))
+    upstream = apply_adjacency([tile_own, tile_other], own, swap(own), False)
+    weight_grad_two, side = second_weight(at, both_cores(pieces_two), all_two)
+    upstream, weight_grad_two, side = exchange_beside(upstream, weight_grad_two, side)
+    weight_grad_two = lax.psum_scatter(weight_grad_two, "col", scatter_dimension=0, tiled=True).astype(F32)
+    grad_pre_one, sums_one, grad_agg_one = first_layer_back(slope_one, weight_one, inverse, upstream, grad_agg_two)
+    own, by_x, by_y = exchange_beside(sums_one, across(grad_pre_one, 1), across(grad_pre_one, 2))
+    cut = nodes // 2
+    plane_one = [grad_pre_one, by_x, by_y, across(by_x[:cut], 2), across(by_y[cut:], 1)]
+    grad_start = exchange(apply_adjacency([tile_own, tile_other], own, swap(own), False))
+    grad_start = input_gradient(grad_start, grad_agg_one, inverse)
+    rights = both_cores(plane_one[:3]) + plane_one[3:] + [swap(part) for part in plane_one[3:]]
+    parts_one = first_weight(at, side, both_cores(pieces_one), rights, cols)
+    weight_grad_one, biases, stats = sum_pieces(over_cols(parts_one))
+    count = full // (2 * chips)
+    bias_grad_two, bias_grad_one = biases[1, :count], biases[0, :count]
+    stats = stats[:, 0]
+    rms_stats = jnp.sqrt(stats[:6].reshape(2, 3) / (stats[6] * full) + 1e-06)
+    return (act, grad_start, weight_grad_one, bias_grad_one, weight_grad_two, bias_grad_two, rms_stats)
+
+
 def solution(mesh):
-    in_specs = (
-        P(("row", "col"), None),
-        P(),
-        P(),
-        P(),
-        P(),
-        P(("row", "col"), None),
-        P("row", None),
-        P(("row", "col")),
-    )
-    out_specs = (
-        P(("row", "col"), None),
-        P(("row", "col"), None),
-        P(("row", "col"), None),
-        P(("row", "col")),
-        P(("row", "col"), None),
-        P(("row", "col")),
-        P(),
-    )
-    return jax.shard_map(local, mesh=mesh, in_specs=in_specs, out_specs=out_specs, check_vma=False)
+    rows, cols = mesh.devices.shape
+    axes = ("ch", "core", "col")
+    wide = Mesh(mesh.devices.reshape(rows // 2, 2, cols), axes)
+
+    def program(features, *rest):
+        nodes, full = features.shape
+        slots = rest[5].shape[1]
+        fits = (
+            (rows, cols) == (8, 4)
+            and nodes == rows * cols * LANES
+            and full == rows * cols * 64
+            and slots * nodes == MXU * MXU
+            and slots == 16
+        )
+        split, over = (axes, wide) if fits else (("row", "col"), mesh)
+        lists = ("ch", "core") if fits else "row"
+        spread = P(split, None)
+        return jax.shard_map(
+            transposed if fits else general,
+            mesh=over,
+            in_specs=(spread, P(), P(), P(), P(), spread, P(lists, None), P(split)),
+            out_specs=(spread, spread, spread, P(split), spread, P(split), P()),
+            check_vma=False,
+        )(features, *rest)
+
+    return program

time: 1290 us -> 311 us (0.24)
  waiting for transfers between devices: 1120 us -> 93.3 us
  Pallas kernels: 0 us -> 104 us
  matrix products: 82.7 us -> 0 us
  starting transfers between devices: 1.07 us -> 75.9 us
  blocking collectives: 41.7 us -> 0 us
    reduce_scatter x6 -> x1, waiting for transfers between devices: 953 us -> 0.01 us  [transposed(): lax.psum_scatter(weight_grad_two, 'col', scatter_dimension=0, tiled=True)]
    all_gather x4 -> x1, waiting for transfers between devices: 166 us -> 7.62 us  [transposed(): all_two = lax.all_gather(grad_pre_two, ('ch', 'core'), axis=0, tiled=True)]
    pallas_call x0 -> x14, Pallas kernels: none -> 104 us  [the longest x3 37.6 us: count_tile(): pl.pallas_call(functools.partial(tile_kernel, turn, nodes, cols), grid=(r...]
    ppermute x0 -> x34, waiting for transfers between devices: none -> 84.1 us  [the longest x13 47.7 us: across(): return lax.ppermute(value, 'ch', [(i, i ^ mask) for i in range(chip_rows)])]
    dot_general x10 -> x0, matrix products: 82.7 us -> none  [the longest x2 21.6 us: backward_layer(): lax.dot_general(front_tile, grad_all, (((0,), (0,)), ((), ())), preferred...]
    all_to_all x0 -> x8, starting transfers between devices: none -> 52.9 us  [exchange(): return lax.all_to_all(value, every, 0, 0, tiled=True)]
    unnamed x1 -> x0, blocking collectives: 41.7 us -> none
    ppermute x0 -> x34, starting transfers between devices: none -> 22.9 us  [the longest x13 15.8 us: across(): return lax.ppermute(value, 'ch', [(i, i ^ mask) for i in range(chip_rows)])]
  transfers between devices with their start and end apart: 10 -> 44, of which waited for: 10 -> 25; matrix products, arithmetic and copies ran while one was open for 2% -> 4% of each run, Pallas kernels for 0% -> 21%
where the time goes in v2:
time: 311 us; the launch traced here: 309 us
  Pallas kernels  104 us (33%)
  waiting for transfers between devices  93.3 us (30%)
  starting transfers between devices  75.9 us (24%)
  local copies, waits for them, and re-layouts  15.8 us (5%)
  between operations  15.1 us (5%)
  other arithmetic  5.07 us (2%)
    all_to_all x8, starting transfers between devices, exchange(): return lax.all_to_all(value, every, 0, 0, tiled=True)  52.9 us
    ppermute x13, waiting for transfers between devices, across(): return lax.ppermute(value, 'ch', [(i, i ^ mask) for i in range(chip_rows)])  47.7 us
    pallas_call x3, Pallas kernels, count_tile(): pl.pallas_call(functools.partial(tile_kernel, turn, nodes, cols), grid=(r...  37.6 us
    ppermute x3, waiting for transfers between devices, over_cols(): lax.ppermute(parts[mask], 'col', [(i, i ^ mask) for i in range(cols)])  27.4 us
    pallas_call x4, Pallas kernels, apply_adjacency(): pl.pallas_call(functools.partial(adjacency_kernel, forward, len(tiles)),...  25.1 us
    ppermute x13, starting transfers between devices, across(): return lax.ppermute(value, 'ch', [(i, i ^ mask) for i in range(chip_rows)])  15.8 us
    unnamed x78, local copies, waits for them, and re-layouts  10.6 us
    pallas_call x1, Pallas kernels, second_layer(): pl.pallas_call(second_kernel, in_specs=[IN_SMEM, IN_ANY, IN_ANY, IN_VMEM,...  9.09 us
  transfers between devices with their start and end apart: 44, of which 25 were waited for; matrix products, arithmetic and copies ran while one was open for 4% of the time, Pallas kernels for 21%

profile of v2, /device:TPU:8, one launch (start us, length us, event | category | flops | bytes accessed | tf_op | source)
XLA Modules:
  0.0 309.2 jit_solution(8995406262475635630)
XLA Ops:
  7.2 0.9 copy.21
  8.2 2.5 collective-permute-start.2
  11.8 1.3 copy.19
  13.1 1.0 copy.20
  14.1 7.2 %all-to-all-start = ((bf16[16,128,128]{2,1,0:T(8,128)(2,1)}), bf16[16,128,128]{2,1,0:T(8,128)(2,1)S(1)}, u32[]{:S(2)}, u32[]{:S(2)}) async-start(bf16[16,128,128]{2,1,0:T(8,128)(2,1)} %bitcast.3), calls=%async_computation | async-start | bytes 1048576 | tf_op jit(solution)/shard_map/all_to_all | solution.py:768
  22.7 14.9 %shard_map.135.refs_0_ = f8e4m3fn[4096,2048]{1,0:T(32,128)(4,1)} custom-call(s32[2]{0:T(128)} %pad_add_fusion.1.place_ref.at_ref, s32[4,32,256]{2,1,0:T(8,128)} %pad_add_fusion.lists_ref), custom_call_target="tpu_custom_call" | custom-call | flops 17179869184 | bytes 4194304 | tf_op jit(solution)/shard_map/pallas_call | solution.py:237
  37.8 1.9 collective-permute-done.3.other_ref
  39.7 0.8 copy-done.12
  40.4 6.4 %shard_map.136 = bf16[16,128,128]{2,1,0:T(8,128)(2,1)} custom-call(bf16[16,128,128]{2,1,0:T(8,128)(2,1)} %copy-done.1, bf16[16,128,128]{2,1,0:T(8,128)(2,1)} %copy-done.12, f8e4m3fn[4096,2048]{1,0:T(32,128)(4,1)} %shard_map.135.refs_0_), custom_call_target="tpu_custom_call" | custom-call | flops 2147483648 | bytes 8388608 | tf_op jit(solution)/shard_map/pallas_call | solution.py:296
  46.8 6.9 %all-to-all-start.1 = ((bf16[16,128,128]{2,1,0:T(8,128)(2,1)}), bf16[16,128,128]{2,1,0:T(8,128)(2,1)S(1)}, u32[]{:S(2)}, u32[]{:S(2)}) async-start(bf16[16,128,128]{2,1,0:T(8,128)(2,1)} %shard_map.136), calls=%async_computation.1 | async-start | bytes 1048576 | tf_op jit(solution)/shard_map/all_to_all | solution.py:768
  54.5 11.3 %shard_map.137.refs_0_ = f8e4m3fn[2048,2048]{1,0:T(32,128)(4,1)} custom-call(s32[2]{0:T(128)} %pad_add_fusion.1.place_ref.at_ref, s32[4,32,256]{2,1,0:T(8,128)} %pad_add_fusion.lists_ref), custom_call_target="tpu_custom_call" | custom-call | flops 8589934592 | bytes 4194304 | tf_op jit(solution)/shard_map/pallas_call | solution.py:237
  65.8 1.5 all-to-all-done.1.agg_ref
  67.3 0.8 copy-done.4
  68.1 7.7 %shard_map.138 = (bf16[16,128,128]{2,1,0:T(8,128)(2,1)}, f32[128,2048]{1,0:T(8,128)}, f32[8,128]{1,0:T(8,128)}, bf16[128,512]{1,0:T(8,128)(2,1)}, bf16[128,512]{...) custom-call(s32[2]{0:T(128)} %pad_add_fusion.1.place_ref.at_ref, bf16[16,128,128]{2,1,0:T(8,128)(2,1)} %copy-done.4, ...), custom_call_target="tpu_custom_call" | custom-call | flops 1073741824 | bytes 8388608 | tf_op jit(solution)/shard_map/pallas_call | solution.py:378
  75.8 6.4 %all-to-all-start.2 = ((bf16[16,128,128]{2,1,0:T(8,128)(2,1)}), bf16[16,128,128]{2,1,0:T(8,128)(2,1)S(1)}, u32[]{:S(2)}, u32[]{:S(2)}) async-start(bf16[16,128,128]{2,1,0:T(8,128)(2,1)} %get-tuple-element.59), calls=%async_computation.2 | async-start | bytes 1048576 | tf_op jit(solution)/shard_map/all_to_all | solution.py:768
  82.3 1.3 collective-permute-done.4.lists_ref
  84.3 11.3 %shard_map.139.refs_1_ = f8e4m3fn[2048,2048]{1,0:T(32,128)(4,1)} custom-call(s32[2]{0:T(128)} %pad_add_fusion.1.place_ref.at_ref, s32[4,32,256]{2,1,0:T(8,128)} %copy-done.36), custom_call_target="tpu_custom_call" | custom-call | flops 8589934592 | bytes 4194304 | tf_op jit(solution)/shard_map/pallas_call | solution.py:237
  95.8 1.8 collective-permute-done.5.other_ref
  97.6 0.8 copy-done.11
  98.4 6.4 %shard_map.140 = bf16[16,128,128]{2,1,0:T(8,128)(2,1)} custom-call(bf16[16,128,128]{2,1,0:T(8,128)(2,1)} %copy-done.3, bf16[16,128,128]{2,1,0:T(8,128)(2,1)} %copy-done.11, f8e4m3fn[4096,2048]{1,0:T(32,128)(4,1)} %shard_map.135.refs_0_), custom_call_target="tpu_custom_call" | custom-call | flops 2147483648 | bytes 8388608 | tf_op jit(solution)/shard_map/pallas_call | solution.py:296
  104.8 7.0 %all-to-all-start.3 = ((bf16[16,128,128]{2,1,0:T(8,128)(2,1)}), bf16[16,128,128]{2,1,0:T(8,128)(2,1)S(1)}, u32[]{:S(2)}, u32[]{:S(2)}) async-start(bf16[16,128,128]{2,1,0:T(8,128)(2,1)} %shard_map.140), calls=%async_computation.3 | async-start | bytes 1048576 | tf_op jit(solution)/shard_map/all_to_all | solution.py:768
  112.5 1.5 collective-permute-start.6
  114.1 1.5 collective-permute-start.7
  116.6 4.7 %collective-permute-done.6.refs_2_ = bf16[128,512]{1,0:T(8,128)(2,1)S(1)} collective-permute-done((bf16[128,512]{1,0:T(8,128)(2,1)S(1)}, bf16[128,512]{1,0:T(8,128)(2,1)S(1)}, u32[]{:S(2)}, u32[]{:S(2)}) %collective-permute-start.6) | collective-permute-done | bytes 131104 | tf_op jit(solution)/shard_map/ppermute | solution.py:765
  121.3 1.4 collective-permute-done.7.refs_4_
  123.3 3.2 %collective-permute-done.8.refs_6_ = bf16[128,512]{1,0:T(8,128)(2,1)} collective-permute-done((bf16[128,512]{1,0:T(8,128)(2,1)S(1)}, bf16[128,512]{1,0:T(8,128)(2,1)}, u32[]{:S(2)}, u32[]{:S(2)}) %collective-permute-start.8) | collective-permute-done | bytes 131104 | tf_op jit(solution)/shard_map/ppermute | solution.py:765
  126.5 0.8 copy-done.7
  127.3 9.1 %shard_map.141 = (bf16[128,2048]{1,0:T(8,128)(2,1)}, bf16[128,2176]{1,0:T(8,128)(2,1)}, bf16[16,128,128]{2,1,0:T(8,128)(2,1)}, bf16[16,128,128]{2,1,0:T(8,128)(2...) custom-call(s32[2]{0:T(128)} %pad_add_fusion.1.place_ref.at_ref, ...), custom_call_target="tpu_custom_call" | custom-call | flops 2147483648 | bytes 8388608 | tf_op jit(solution)/shard_map/pallas_call | solution.py:466
  136.4 5.9 %all-to-all-start.4 = ((bf16[16,128,128]{2,1,0:T(8,128)(2,1)}), bf16[16,128,128]{2,1,0:T(8,128)(2,1)S(1)}, u32[]{:S(2)}, u32[]{:S(2)}) async-start(bf16[16,128,128]{2,1,0:T(8,128)(2,1)} %get-tuple-element.69), calls=%async_computation.4 | async-start | bytes 1048576 | tf_op jit(solution)/shard_map/all_to_all | solution.py:768
  142.3 1.5 collective-permute-start.9
  143.8 1.5 collective-permute-start.10
  145.8 11.0 %collective-permute-done.9.refs_2_ = bf16[128,512]{1,0:T(8,128)(2,1)S(1)} collective-permute-done((bf16[128,512]{1,0:T(8,128)(2,1)}, bf16[128,512]{1,0:T(8,128)(2,1)S(1)}, u32[]{:S(2)}, u32[]{:S(2)}) %collective-permute-start.9) | collective-permute-done | bytes 131104 | tf_op jit(solution)/shard_map/ppermute | solution.py:765
  156.9 4.5 %collective-permute-done.11.refs_6_ = bf16[128,512]{1,0:T(8,128)(2,1)S(1)} collective-permute-done((bf16[128,512]{1,0:T(8,128)(2,1)}, bf16[128,512]{1,0:T(8,128)(2,1)S(1)}, u32[]{:S(2)}, u32[]{:S(2)}) %collective-permute-start.11) | collective-permute-done | bytes 131104 | tf_op jit(solution)/shard_map/ppermute | solution.py:765
  161.5 1.9 collective-permute-done.12.other_ref
  163.4 0.8 copy-done.13
  164.2 6.5 %shard_map.142 = bf16[16,128,128]{2,1,0:T(8,128)(2,1)} custom-call(bf16[16,128,128]{2,1,0:T(8,128)(2,1)} %copy-done.2, bf16[16,128,128]{2,1,0:T(8,128)(2,1)} %copy-done.13, f8e4m3fn[2048,2048]{1,0:T(32,128)(4,1)} %shard_map.137.refs_0_, f8e4m3fn[2048,2048]{1,0:T(32,128)(4,1)} %shard_map.139.refs_1_), custom_call_target="tpu_custom_call" | custom-call | flops 2147483648 | bytes 8388608 | tf_op jit(solution)/shard_map/pallas_call | solution.py:296
  170.7 5.1 %all-to-all-start.5 = ((bf16[16,128,128]{2,1,0:T(8,128)(2,1)}), bf16[16,128,128]{2,1,0:T(8,128)(2,1)S(1)}, u32[]{:S(2)}, u32[]{:S(2)}) async-start(bf16[16,128,128]{2,1,0:T(8,128)(2,1)} %shard_map.142), calls=%async_computation.5 | async-start | bytes 1048576 | tf_op jit(solution)/shard_map/all_to_all | solution.py:768
  178.0 7.6 %all-gather.2.cloned.1.call-done.refs_8_ = bf16[1024,2176]{1,0:T(8,128)(2,1)} async-done(((bf16[128,2176]{1,0:T(8,128)(2,1)}), bf16[1024,2176]{1,0:T(8,128)(2,1)}) %all-gather.2.cloned.1.call-update) | async-done | bytes 4456464 | tf_op jit(solution)/shard_map/all_gather | solution.py:810
  185.6 5.9 %shard_map.143 = (bf16[256,2048]{1,0:T(8,128)(2,1)}, f32[16,256]{1,0:T(8,128)}) custom-call(s32[2]{0:T(128)} %pad_add_fusion.1.place_ref.at_ref, bf16[128,512]{1,0:T(8,128)(2,1)} %get-tuple-element.77.refs_0_, bf16[128,512]{1,0:T(8,128)(2,1)} %copy-done.28, bf16[128,512]{1,0:T(8,128)(2,1)} %copy-done.25, bf16[128,512]{1,0:T(8,128)(2,1)} %copy-done.29, ...), custom_call_target="tpu_custom_call" | custom-call | flops 1073741824 | bytes 8388608 | tf_op jit(solution)/shard_map/pallas_call | solution.py:616
  191.5 0.8 copy-done.6
  192.3 8.2 %shard_map.144 = (bf16[128,2176]{1,0:T(8,128)(2,1)}, bf16[16,128,128]{2,1,0:T(8,128)(2,1)}, bf16[16,128,128]{2,1,0:T(8,128)(2,1)}) custom-call(f32[128,2048]{1,0:T(8,128)} %get-tuple-element.68.slope_ref, bf16[2048,2048]{1,0:T(8,128)(2,1)} %weight_ref.5, f32[1,128]{1,0:T(1,128)} %divide_bitcast_fusion.inverse_ref, bf16[16,128,128]{2,1,0:T(8,128)(2,1)} %copy-done.6, ...), custom_call_target="tpu_custom_call" | custom-call | flops 1073741824 | bytes 8388608 | tf_op jit(solution)/shard_map/pallas_call | solution.py:523
  200.6 8.3 %all-to-all-start.6 = ((bf16[16,128,128]{2,1,0:T(8,128)(2,1)}), bf16[16,128,128]{2,1,0:T(8,128)(2,1)S(1)}, u32[]{:S(2)}, u32[]{:S(2)}) async-start(bf16[16,128,128]{2,1,0:T(8,128)(2,1)} %get-tuple-element.86), calls=%async_computation.6 | async-start | bytes 1048576 | tf_op jit(solution)/shard_map/all_to_all | solution.py:768
  208.9 1.5 collective-permute-start.18
  210.5 1.5 collective-permute-start.17
  212.0 16.8 %collective-permute-done.18.refs_12_ = bf16[128,2176]{1,0:T(8,128)(2,1)S(1)} collective-permute-done((bf16[128,2176]{1,0:T(8,128)(2,1)}, bf16[128,2176]{1,0:T(8,128)(2,1)S(1)}, u32[]{:S(2)}, u32[]{:S(2)}) %collective-permute-start.18) | collective-permute-done | bytes 557088 | tf_op jit(solution)/shard_map/ppermute | solution.py:765
  229.1 1.3 collective-permute-start.28
  230.9 0.9 collective-permute-start.27
  232.4 1.0 collective-permute-done.22.refs_5_
  234.0 4.2 %collective-permute-done.28.refs_15_ = bf16[64,2176]{1,0:T(8,128)(2,1)S(1)} collective-permute-done((bf16[64,2176]{1,0:T(8,128)(2,1)S(1)}, bf16[64,2176]{1,0:T(8,128)(2,1)S(1)}, u32[]{:S(2)}, u32[]{:S(2)}) %collective-permute-start.28) | collective-permute-done | bytes 278560 | tf_op jit(solution)/shard_map/ppermute | solution.py:765
  238.2 1.6 collective-permute-done.27.refs_14_
  241.2 5.9 %shard_map.145 = bf16[16,128,128]{2,1,0:T(8,128)(2,1)} custom-call(bf16[16,128,128]{2,1,0:T(8,128)(2,1)} %copy-done, bf16[16,128,128]{2,1,0:T(8,128)(2,1)} %copy-done.10, f8e4m3fn[2048,2048]{1,0:T(32,128)(4,1)} %shard_map.137.refs_0_, f8e4m3fn[2048,2048]{1,0:T(32,128)(4,1)} %shard_map.139.refs_1_), custom_call_target="tpu_custom_call" | custom-call | flops 2147483648 | bytes 8388608 | tf_op jit(solution)/shard_map/pallas_call | solution.py:296
  247.1 6.0 %all-to-all-start.7 = ((bf16[16,128,128]{2,1,0:T(8,128)(2,1)}), bf16[16,128,128]{2,1,0:T(8,128)(2,1)S(1)}, u32[]{:S(2)}, u32[]{:S(2)}) async-start(bf16[16,128,128]{2,1,0:T(8,128)(2,1)} %shard_map.145), calls=%async_computation.7 | async-start | bytes 1048576 | tf_op jit(solution)/shard_map/all_to_all | solution.py:768
  253.1 6.0 %shard_map.147 = (bf16[64,2176]{1,0:T(8,128)(2,1)}, bf16[64,2176]{1,0:T(8,128)(2,1)}, bf16[64,2176]{1,0:T(8,128)(2,1)}, bf16[64,2176]{1,0:T(8,128)(2,1)}) custom-call(s32[2]{0:T(128)} %pad_add_fusion.1.place_ref.at_ref, f32[16,256]{1,0:T(8,128)} %get-tuple-element.90.side_ref, bf16[128,512]{1,0:T(8,128)(2,1)} %get-tuple-element.91.refs_0_, ...), custom_call_target="tpu_custom_call" | custom-call | flops 1073741824 | bytes 8388608 | tf_op jit(solution)/shard_map/pallas_call | solution.py:688
  259.4 2.8 collective-permute-start.32
  262.7 9.7 %collective-permute-done.31.refs_1_ = bf16[64,2176]{1,0:T(8,128)(2,1)S(1)} collective-permute-done((bf16[64,2176]{1,0:T(8,128)(2,1)}, bf16[64,2176]{1,0:T(8,128)(2,1)S(1)}, u32[]{:S(2)}, u32[]{:S(2)}) %collective-permute-start.31) | collective-permute-done | bytes 278560 | tf_op jit(solution)/shard_map/ppermute | solution.py:792
  272.4 9.9 %collective-permute-done.32.refs_2_ = bf16[64,2176]{1,0:T(8,128)(2,1)S(1)} collective-permute-done((bf16[64,2176]{1,0:T(8,128)(2,1)}, bf16[64,2176]{1,0:T(8,128)(2,1)S(1)}, u32[]{:S(2)}, u32[]{:S(2)}) %collective-permute-start.32) | collective-permute-done | bytes 278560 | tf_op jit(solution)/shard_map/ppermute | solution.py:792
  282.3 7.8 %collective-permute-done.33.refs_3_ = bf16[64,2176]{1,0:T(8,128)(2,1)S(1)} collective-permute-done((bf16[64,2176]{1,0:T(8,128)(2,1)}, bf16[64,2176]{1,0:T(8,128)(2,1)S(1)}, u32[]{:S(2)}, u32[]{:S(2)}) %collective-permute-start.33) | collective-permute-done | bytes 278560 | tf_op jit(solution)/shard_map/ppermute | solution.py:792
  290.8 2.1 shard_map.148
  293.0 1.2 slice.28
  294.8 0.8 sqrt_reduce_fusion
  296.3 1.3 slice_bitcast_fusion
  297.5 1.8 convert_element_type.23
  299.3 0.8 copy-done.5
  300.1 2.3 shard_map.146
  (134 shorter events, 15.3 us)
Async XLA Ops:
  8.2 13.8 %collective-permute-start.2 = (s32[32,256]{1,0:T(8,128)S(1)}, s32[32,256]{1,0:T(8,128)S(1)}, u32[]{:S(2)}, u32[]{:S(2)}) collective-permute-start(s32[32,256]{1,0:T(8,128)S(1)} %reshape.69), channel_id=1, source_target_pairs={{0,24},{8,16},{16,8},{24,0},{1,25},{9,17},{17,9},{25,1},{2,26},{10... | collective-permute-start | bytes 98312 | tf_op jit(solution)/shard_map/ppermute | solution.py:765
  10.7 11.3 %collective-permute-start.1 = (s32[32,256]{1,0:T(8,128)S(1)}, s32[32,256]{1,0:T(8,128)S(1)}, u32[]{:S(2)}, u32[]{:S(2)}) collective-permute-start(s32[32,256]{1,0:T(8,128)S(1)} %reshape.69), channel_id=1, source_target_pairs={{0,16},{8,24},{16,0},{24,8},{1,17},{9,25},{17,1},{25,9},{2,18},{10... | collective-permute-start | bytes 98312 | tf_op jit(solution)/shard_map/ppermute | solution.py:765
  11.2 10.8 %collective-permute-start = (s32[32,256]{1,0:T(8,128)S(1)}, s32[32,256]{1,0:T(8,128)S(1)}, u32[]{:S(2)}, u32[]{:S(2)}) collective-permute-start(s32[32,256]{1,0:T(8,128)S(1)} %reshape.69), channel_id=1, source_target_pairs={{0,8},{8,0},{16,24},{24,16},{1,9},{9,1},{17,25},{25,17},{2,10},{10... | collective-permute-start | bytes 98312 | tf_op jit(solution)/shard_map/ppermute | solution.py:765
  14.1 23.6 %all-to-all-start = ((bf16[16,128,128]{2,1,0:T(8,128)(2,1)}), bf16[16,128,128]{2,1,0:T(8,128)(2,1)S(1)}, u32[]{:S(2)}, u32[]{:S(2)}) async-start(bf16[16,128,128]{2,1,0:T(8,128)(2,1)} %bitcast.3), calls=%async_computation | async-start | bytes 1048576 | tf_op jit(solution)/shard_map/all_to_all | solution.py:768
  37.7 16.1 %copy-start.37 = (s32[128]{0:T(128)S(1)}, s32[128]{0:T(128)}, u32[]{:S(2)}) copy-start(s32[128]{0:T(128)} %param.15) | copy-start | bytes 1540
  37.7 2.0 collective-permute-start.3
  46.8 20.4 %all-to-all-start.1 = ((bf16[16,128,128]{2,1,0:T(8,128)(2,1)}), bf16[16,128,128]{2,1,0:T(8,128)(2,1)S(1)}, u32[]{:S(2)}, u32[]{:S(2)}) async-start(bf16[16,128,128]{2,1,0:T(8,128)(2,1)} %shard_map.136), calls=%async_computation.1 | async-start | bytes 1048576 | tf_op jit(solution)/shard_map/all_to_all | solution.py:768
  65.8 16.4 %copy-start.32 = (s32[4,32,256]{2,1,0:T(8,128)S(1)}, s32[4,32,256]{2,1,0:T(8,128)}, u32[]{:S(2)}) copy-start(s32[4,32,256]{2,1,0:T(8,128)} %pad_add_fusion.lists_ref) | copy-start | bytes 393220
  75.8 19.9 %all-to-all-start.2 = ((bf16[16,128,128]{2,1,0:T(8,128)(2,1)}), bf16[16,128,128]{2,1,0:T(8,128)(2,1)S(1)}, u32[]{:S(2)}, u32[]{:S(2)}) async-start(bf16[16,128,128]{2,1,0:T(8,128)(2,1)} %get-tuple-element.59), calls=%async_computation.2 | async-start | bytes 1048576 | tf_op jit(solution)/shard_map/all_to_all | solution.py:768
  82.2 1.4 collective-permute-start.4
  95.6 16.9 %copy-start.35 = (bf16[128,512]{1,0:T(8,128)(2,1)S(1)}, bf16[128,512]{1,0:T(8,128)(2,1)}, u32[]{:S(2)}) copy-start(bf16[128,512]{1,0:T(8,128)(2,1)} %get-tuple-element.62) | copy-start | bytes 393220
  95.6 18.5 %copy-start.34 = (bf16[128,512]{1,0:T(8,128)(2,1)S(1)}, bf16[128,512]{1,0:T(8,128)(2,1)}, u32[]{:S(2)}) copy-start(bf16[128,512]{1,0:T(8,128)(2,1)} %get-tuple-element.63) | copy-start | bytes 393220
  95.6 19.9 %copy-start.33 = (bf16[128,512]{1,0:T(8,128)(2,1)S(1)}, bf16[128,512]{1,0:T(8,128)(2,1)}, u32[]{:S(2)}) copy-start(bf16[128,512]{1,0:T(8,128)(2,1)} %get-tuple-element.64) | copy-start | bytes 393220
  95.6 2.0 collective-permute-start.5
  104.8 21.7 %all-to-all-start.3 = ((bf16[16,128,128]{2,1,0:T(8,128)(2,1)}), bf16[16,128,128]{2,1,0:T(8,128)(2,1)S(1)}, u32[]{:S(2)}, u32[]{:S(2)}) async-start(bf16[16,128,128]{2,1,0:T(8,128)(2,1)} %shard_map.140), calls=%async_computation.3 | async-start | bytes 1048576 | tf_op jit(solution)/shard_map/all_to_all | solution.py:768
  111.8 73.8 %all-gather.2.cloned.1.call-start = ((), (), s32[]{:S(2)}) async-start(), calls=%async_computation.9 | async-start | bytes 5013504 | tf_op jit(solution)/shard_map/all_gather | solution.py:810
  112.5 8.8 %collective-permute-start.6 = (bf16[128,512]{1,0:T(8,128)(2,1)S(1)}, bf16[128,512]{1,0:T(8,128)(2,1)S(1)}, u32[]{:S(2)}, u32[]{:S(2)}) collective-permute-start(bf16[128,512]{1,0:T(8,128)(2,1)S(1)} %copy-done.35), channel_id=1, source_target_pairs={{0,8},{8,0},{16,24},{24,16},{1,9},{9,1},{17,25},{25,17},{2,10},{10... | collective-permute-start | bytes 393224 | tf_op jit(solution)/shard_map/ppermute | solution.py:765
  114.1 8.6 %collective-permute-start.7 = (bf16[128,512]{1,0:T(8,128)(2,1)S(1)}, bf16[128,512]{1,0:T(8,128)(2,1)S(1)}, u32[]{:S(2)}, u32[]{:S(2)}) collective-permute-start(bf16[128,512]{1,0:T(8,128)(2,1)S(1)} %copy-done.34), channel_id=1, source_target_pairs={{0,16},{8,24},{16,0},{24,8},{1,17},{9,25},{17,1},{25,9},{2,18},{10... | collective-permute-start | bytes 393224 | tf_op jit(solution)/shard_map/ppermute | solution.py:765
  115.5 11.0 %collective-permute-start.8 = (bf16[128,512]{1,0:T(8,128)(2,1)S(1)}, bf16[128,512]{1,0:T(8,128)(2,1)}, u32[]{:S(2)}, u32[]{:S(2)}) collective-permute-start(bf16[128,512]{1,0:T(8,128)(2,1)S(1)} %copy-done.33), channel_id=1, source_target_pairs={{0,24},{8,16},{16,8},{24,0},{1,25},{9,17},{17,9},{25,1},{2,26},{10... | collective-permute-start | bytes 393224 | tf_op jit(solution)/shard_map/ppermute | solution.py:765
  136.4 39.4 %copy-start.21 = (bf16[128,512]{1,0:T(8,128)(2,1)S(1)}, bf16[128,512]{1,0:T(8,128)(2,1)}, u32[]{:S(2)}) copy-start(bf16[128,512]{1,0:T(8,128)(2,1)} %get-tuple-element.77.refs_0_) | copy-start | bytes 393220
  136.4 25.0 %all-to-all-start.4 = ((bf16[16,128,128]{2,1,0:T(8,128)(2,1)}), bf16[16,128,128]{2,1,0:T(8,128)(2,1)S(1)}, u32[]{:S(2)}, u32[]{:S(2)}) async-start(bf16[16,128,128]{2,1,0:T(8,128)(2,1)} %get-tuple-element.69), calls=%async_computation.4 | async-start | bytes 1048576 | tf_op jit(solution)/shard_map/all_to_all | solution.py:768
  142.3 14.5 %collective-permute-start.9 = (bf16[128,512]{1,0:T(8,128)(2,1)}, bf16[128,512]{1,0:T(8,128)(2,1)S(1)}, u32[]{:S(2)}, u32[]{:S(2)}) collective-permute-start(bf16[128,512]{1,0:T(8,128)(2,1)} %get-tuple-element.71), channel_id=1, source_target_pairs={{0,8},{8,0},{16,24},{24,16},{1,9},{9,1},{17,25},{25,17},{2,10},{10... | collective-permute-start | bytes 393224 | tf_op jit(solution)/shard_map/ppermute | solution.py:765
  143.8 13.1 %collective-permute-start.10 = (bf16[128,512]{1,0:T(8,128)(2,1)}, bf16[128,512]{1,0:T(8,128)(2,1)S(1)}, u32[]{:S(2)}, u32[]{:S(2)}) collective-permute-start(bf16[128,512]{1,0:T(8,128)(2,1)} %get-tuple-element.72), channel_id=1, source_target_pairs={{0,16},{8,24},{16,0},{24,8},{1,17},{9,25},{17,1},{25,9},{2,18},{10... | collective-permute-start | bytes 393224 | tf_op jit(solution)/shard_map/ppermute | solution.py:765
  145.2 16.2 %collective-permute-start.11 = (bf16[128,512]{1,0:T(8,128)(2,1)}, bf16[128,512]{1,0:T(8,128)(2,1)S(1)}, u32[]{:S(2)}, u32[]{:S(2)}) collective-permute-start(bf16[128,512]{1,0:T(8,128)(2,1)} %get-tuple-element.73), channel_id=1, source_target_pairs={{0,24},{8,16},{16,8},{24,0},{1,25},{9,17},{17,9},{25,1},{2,26},{10... | collective-permute-start | bytes 393224 | tf_op jit(solution)/shard_map/ppermute | solution.py:765
  156.8 28.8 %copy-start.25 = (bf16[128,512]{1,0:T(8,128)(2,1)}, bf16[128,512]{1,0:T(8,128)(2,1)S(1)}, u32[]{:S(2)}) copy-start(bf16[128,512]{1,0:T(8,128)(2,1)S(1)} %collective-permute-done.9.refs_2_) | copy-start | bytes 393220
  156.9 28.7 %copy-start.26 = (bf16[128,512]{1,0:T(8,128)(2,1)}, bf16[128,512]{1,0:T(8,128)(2,1)S(1)}, u32[]{:S(2)}) copy-start(bf16[128,512]{1,0:T(8,128)(2,1)S(1)} %collective-permute-done.10.refs_4_) | copy-start | bytes 393220
  161.4 24.2 %copy-start.27 = (bf16[128,512]{1,0:T(8,128)(2,1)}, bf16[128,512]{1,0:T(8,128)(2,1)S(1)}, u32[]{:S(2)}) copy-start(bf16[128,512]{1,0:T(8,128)(2,1)S(1)} %collective-permute-done.11.refs_6_) | copy-start | bytes 393220
  161.4 2.0 collective-permute-start.12
  170.7 20.8 %all-to-all-start.5 = ((bf16[16,128,128]{2,1,0:T(8,128)(2,1)}), bf16[16,128,128]{2,1,0:T(8,128)(2,1)S(1)}, u32[]{:S(2)}, u32[]{:S(2)}) async-start(bf16[16,128,128]{2,1,0:T(8,128)(2,1)} %shard_map.142), calls=%async_computation.5 | async-start | bytes 1048576 | tf_op jit(solution)/shard_map/all_to_all | solution.py:768
  175.8 1.4 collective-permute-start.13
  175.9 1.5 collective-permute-start.14
  176.4 1.3 collective-permute-start.15
  176.5 1.5 collective-permute-start.16
  177.3 8.3 %copy-start.28 = (bf16[128,512]{1,0:T(8,128)(2,1)}, bf16[128,512]{1,0:T(8,128)(2,1)S(1)}, u32[]{:S(2)}) copy-start(bf16[128,512]{1,0:T(8,128)(2,1)S(1)} %collective-permute-done.13.refs_1_) | copy-start | bytes 393220
  177.4 8.2 %copy-start.29 = (bf16[128,512]{1,0:T(8,128)(2,1)}, bf16[128,512]{1,0:T(8,128)(2,1)S(1)}, u32[]{:S(2)}) copy-start(bf16[128,512]{1,0:T(8,128)(2,1)S(1)} %collective-permute-done.14.refs_3_) | copy-start | bytes 393220
  177.8 7.8 %copy-start.30 = (bf16[128,512]{1,0:T(8,128)(2,1)}, bf16[128,512]{1,0:T(8,128)(2,1)S(1)}, u32[]{:S(2)}) copy-start(bf16[128,512]{1,0:T(8,128)(2,1)S(1)} %collective-permute-done.15.refs_5_) | copy-start | bytes 393220
  200.6 28.4 %all-to-all-start.6 = ((bf16[16,128,128]{2,1,0:T(8,128)(2,1)}), bf16[16,128,128]{2,1,0:T(8,128)(2,1)S(1)}, u32[]{:S(2)}, u32[]{:S(2)}) async-start(bf16[16,128,128]{2,1,0:T(8,128)(2,1)} %get-tuple-element.86), calls=%async_computation.6 | async-start | bytes 1048576 | tf_op jit(solution)/shard_map/all_to_all | solution.py:768
  208.9 88.6 %reduce-scatter.2.cloned.1.call-start = ((), (), s32[]{:S(2)}) async-start(), calls=%async_computation.10 | async-start | bytes 1310720 | tf_op jit(solution)/shard_map/reduce_scatter | solution.py:815
  208.9 19.8 %collective-permute-start.18 = (bf16[128,2176]{1,0:T(8,128)(2,1)}, bf16[128,2176]{1,0:T(8,128)(2,1)S(1)}, u32[]{:S(2)}, u32[]{:S(2)}) collective-permute-start(bf16[128,2176]{1,0:T(8,128)(2,1)} %get-tuple-element.87.refs_8_), channel_id=1, source_target_pairs={{0,16},{8,24},{16,0},{24,8},{1,17},{9,25},{17,1},{25,9},{2,18},{10... | collective-permute-start | bytes 1671176 | tf_op jit(solution)/shard_map/ppermute | solution.py:765
  210.5 18.5 %collective-permute-start.17 = (bf16[128,2176]{1,0:T(8,128)(2,1)}, bf16[128,2176]{1,0:T(8,128)(2,1)S(1)}, u32[]{:S(2)}, u32[]{:S(2)}) collective-permute-start(bf16[128,2176]{1,0:T(8,128)(2,1)} %get-tuple-element.87.refs_8_), channel_id=1, source_target_pairs={{0,8},{8,0},{16,24},{24,16},{1,9},{9,1},{17,25},{25,17},{2,10},{10... | collective-permute-start | bytes 1671176 | tf_op jit(solution)/shard_map/ppermute | solution.py:765
  228.7 24.4 %copy-start.8 = (bf16[128,2176]{1,0:T(8,128)(2,1)}, bf16[128,2176]{1,0:T(8,128)(2,1)S(1)}, u32[]{:S(2)}) copy-start(bf16[128,2176]{1,0:T(8,128)(2,1)S(1)} %collective-permute-done.18.refs_12_) | copy-start | bytes 1671172
  229.0 24.2 %copy-start.9 = (bf16[128,2176]{1,0:T(8,128)(2,1)}, bf16[128,2176]{1,0:T(8,128)(2,1)S(1)}, u32[]{:S(2)}) copy-start(bf16[128,2176]{1,0:T(8,128)(2,1)S(1)} %collective-permute-done.17.refs_10_) | copy-start | bytes 1671172
  229.0 12.2 %copy-start = (bf16[16,128,128]{2,1,0:T(8,128)(2,1)}, bf16[16,128,128]{2,1,0:T(8,128)(2,1)S(1)}, u32[]{:S(2)}) copy-start(bf16[16,128,128]{2,1,0:T(8,128)(2,1)S(1)} %all-to-all-done.6.own_ref) | copy-start | bytes 1572868
  229.0 10.9 %collective-permute-start.19 = (bf16[16,128,128]{2,1,0:T(8,128)(2,1)S(1)}, bf16[16,128,128]{2,1,0:T(8,128)(2,1)S(1)}, u32[]{:S(2)}, u32[]{:S(2)}) collective-permute-start(bf16[16,128,128]{2,1,0:T(8,128)(2,1)S(1)} %all-to-all-done.6.own_ref), channel_id=1, source_target_pairs={{0,4},{4,0},{1,5},{5,1},{2,6},{6,2},{3,7},{7,3},{8,12},{12,8},{9,1... | collective-permute-start | bytes 1572872 | tf_op jit(solution)/shard_map/ppermute | solution.py:762
  229.1 9.1 %collective-permute-start.28 = (bf16[64,2176]{1,0:T(8,128)(2,1)S(1)}, bf16[64,2176]{1,0:T(8,128)(2,1)S(1)}, u32[]{:S(2)}, u32[]{:S(2)}) collective-permute-start(bf16[64,2176]{1,0:T(8,128)(2,1)S(1)} %slice.24), channel_id=1, source_target_pairs={{0,8},{8,0},{16,24},{24,16},{1,9},{9,1},{17,25},{25,17},{2,10},{10... | collective-permute-start | bytes 835592 | tf_op jit(solution)/shard_map/ppermute | solution.py:765
  230.3 1.6 collective-permute-start.20
  230.6 1.6 collective-permute-start.21
  230.9 8.9 %collective-permute-start.27 = (bf16[64,2176]{1,0:T(8,128)(2,1)S(1)}, bf16[64,2176]{1,0:T(8,128)(2,1)}, u32[]{:S(2)}, u32[]{:S(2)}) collective-permute-start(bf16[64,2176]{1,0:T(8,128)(2,1)S(1)} %slice.23), channel_id=1, source_target_pairs={{0,16},{8,24},{16,0},{24,8},{1,17},{9,25},{17,1},{25,9},{2,18},{10... | collective-permute-start | bytes 835592 | tf_op jit(solution)/shard_map/ppermute | solution.py:765
  231.9 7.9 %copy-start.20 = (bf16[128,512]{1,0:T(8,128)(2,1)}, bf16[128,512]{1,0:T(8,128)(2,1)S(1)}, u32[]{:S(2)}) copy-start(bf16[128,512]{1,0:T(8,128)(2,1)S(1)} %collective-permute-done.20.refs_1_) | copy-start | bytes 393220
  231.9 1.6 collective-permute-start.22
  232.1 7.7 %copy-start.22 = (bf16[128,512]{1,0:T(8,128)(2,1)}, bf16[128,512]{1,0:T(8,128)(2,1)S(1)}, u32[]{:S(2)}) copy-start(bf16[128,512]{1,0:T(8,128)(2,1)S(1)} %collective-permute-done.21.refs_3_) | copy-start | bytes 393220
  232.1 1.6 collective-permute-start.23
  233.5 19.6 %collective-permute-start.24 = (bf16[128,2176]{1,0:T(8,128)(2,1)}, bf16[128,2176]{1,0:T(8,128)(2,1)}, u32[]{:S(2)}, u32[]{:S(2)}) collective-permute-start(bf16[128,2176]{1,0:T(8,128)(2,1)} %get-tuple-element.87.refs_8_), channel_id=1, source_target_pairs={{0,4},{4,0},{1,5},{5,1},{2,6},{6,2},{3,7},{7,3},{8,12},{12,8},{9,1... | collective-permute-start | bytes 1671176 | tf_op jit(solution)/shard_map/ppermute | solution.py:762
  233.7 19.4 %collective-permute-start.25 = (bf16[128,2176]{1,0:T(8,128)(2,1)S(1)}, bf16[128,2176]{1,0:T(8,128)(2,1)}, u32[]{:S(2)}, u32[]{:S(2)}) collective-permute-start(bf16[128,2176]{1,0:T(8,128)(2,1)S(1)} %collective-permute-done.17.refs_10_), channel_id=1, source_target_pairs={{0,4},{4,0},{1,5},{5,1},{2,6},{6,2},{3,7},{7,3},{8,12},{12,8},{9,1... | collective-permute-start | bytes 1671176 | tf_op jit(solution)/shard_map/ppermute | solution.py:762
  238.2 14.9 %copy-start.14 = (bf16[64,2176]{1,0:T(8,128)(2,1)}, bf16[64,2176]{1,0:T(8,128)(2,1)S(1)}, u32[]{:S(2)}) copy-start(bf16[64,2176]{1,0:T(8,128)(2,1)S(1)} %collective-permute-done.28.refs_15_) | copy-start | bytes 835588
  238.2 14.9 %collective-permute-start.26 = (bf16[128,2176]{1,0:T(8,128)(2,1)S(1)}, bf16[128,2176]{1,0:T(8,128)(2,1)}, u32[]{:S(2)}, u32[]{:S(2)}) collective-permute-start(bf16[128,2176]{1,0:T(8,128)(2,1)S(1)} %collective-permute-done.18.refs_12_), channel_id=1, source_target_pairs={{0,4},{4,0},{1,5},{5,1},{2,6},{6,2},{3,7},{7,3},{8,12},{12,8},{9,1... | collective-permute-start | bytes 1671176 | tf_op jit(solution)/shard_map/ppermute | solution.py:762
  239.8 13.3 %collective-permute-start.30 = (bf16[64,2176]{1,0:T(8,128)(2,1)S(1)}, bf16[64,2176]{1,0:T(8,128)(2,1)}, u32[]{:S(2)}, u32[]{:S(2)}) collective-permute-start(bf16[64,2176]{1,0:T(8,128)(2,1)S(1)} %collective-permute-done.28.refs_15_), channel_id=1, source_target_pairs={{0,4},{4,0},{1,5},{5,1},{2,6},{6,2},{3,7},{7,3},{8,12},{12,8},{9,1... | collective-permute-start | bytes 835592 | tf_op jit(solution)/shard_map/ppermute | solution.py:762
  240.7 12.4 %collective-permute-start.29 = (bf16[64,2176]{1,0:T(8,128)(2,1)}, bf16[64,2176]{1,0:T(8,128)(2,1)}, u32[]{:S(2)}, u32[]{:S(2)}) collective-permute-start(bf16[64,2176]{1,0:T(8,128)(2,1)} %collective-permute-done.27.refs_14_), channel_id=1, source_target_pairs={{0,4},{4,0},{1,5},{5,1},{2,6},{6,2},{3,7},{7,3},{8,12},{12,8},{9,1... | collective-permute-start | bytes 835592 | tf_op jit(solution)/shard_map/ppermute | solution.py:762
  247.1 52.3 %all-to-all-start.7 = ((bf16[16,128,128]{2,1,0:T(8,128)(2,1)}), bf16[16,128,128]{2,1,0:T(8,128)(2,1)S(1)}, u32[]{:S(2)}, u32[]{:S(2)}) async-start(bf16[16,128,128]{2,1,0:T(8,128)(2,1)} %shard_map.145), calls=%async_computation.7 | async-start | bytes 1048576 | tf_op jit(solution)/shard_map/all_to_all | solution.py:768
  259.2 13.2 %collective-permute-start.31 = (bf16[64,2176]{1,0:T(8,128)(2,1)}, bf16[64,2176]{1,0:T(8,128)(2,1)S(1)}, u32[]{:S(2)}, u32[]{:S(2)}) collective-permute-start(bf16[64,2176]{1,0:T(8,128)(2,1)} %get-tuple-element.98), channel_id=1, source_target_pairs={{0,1},{1,0},{2,3},{3,2},{4,5},{5,4},{6,7},{7,6},{8,9},{9,8},{10,11... | collective-permute-start | bytes 835592 | tf_op jit(solution)/shard_map/ppermute | solution.py:792
  259.4 23.0 %collective-permute-start.32 = (bf16[64,2176]{1,0:T(8,128)(2,1)}, bf16[64,2176]{1,0:T(8,128)(2,1)S(1)}, u32[]{:S(2)}, u32[]{:S(2)}) collective-permute-start(bf16[64,2176]{1,0:T(8,128)(2,1)} %get-tuple-element.99), channel_id=1, source_target_pairs={{0,2},{1,3},{2,0},{3,1},{4,6},{5,7},{6,4},{7,5},{8,10},{9,11},{10,... | collective-permute-start | bytes 835592 | tf_op jit(solution)/shard_map/ppermute | solution.py:792
  262.2 28.0 %collective-permute-start.33 = (bf16[64,2176]{1,0:T(8,128)(2,1)}, bf16[64,2176]{1,0:T(8,128)(2,1)S(1)}, u32[]{:S(2)}, u32[]{:S(2)}) collective-permute-start(bf16[64,2176]{1,0:T(8,128)(2,1)} %get-tuple-element.100), channel_id=1, source_target_pairs={{0,3},{1,2},{2,1},{3,0},{4,7},{5,6},{6,5},{7,4},{8,11},{9,10},{10,... | collective-permute-start | bytes 835592 | tf_op jit(solution)/shard_map/ppermute | solution.py:792
  272.4 17.7 %copy-start.15 = (bf16[64,2176]{1,0:T(8,128)(2,1)}, bf16[64,2176]{1,0:T(8,128)(2,1)S(1)}, u32[]{:S(2)}) copy-start(bf16[64,2176]{1,0:T(8,128)(2,1)S(1)} %collective-permute-done.31.refs_1_) | copy-start | bytes 835588
  282.3 7.8 %copy-start.16 = (bf16[64,2176]{1,0:T(8,128)(2,1)}, bf16[64,2176]{1,0:T(8,128)(2,1)S(1)}, u32[]{:S(2)}) copy-start(bf16[64,2176]{1,0:T(8,128)(2,1)S(1)} %collective-permute-done.32.refs_2_) | copy-start | bytes 835588
  (18 other events, 35.9 us)
Sparse Core Ops, SparseCore 0:
  136.5 48.9 all-gather.1
  212.1 28.0 reduce-scatter.1
